TPU v7x, 128 devices: a whole 4x4x4 slice. The times are simulated.
128 devices in a mesh: sta: 8 (over z, y_hi), day: 16 (over x, y_lo, core).
Axes of the slice: x: 4, y: 4 (y_hi: 2, y_lo: 2; y = y_hi * 2 + y_lo), z: 4, core: 2. Of those that a mesh axis runs over, the one named last changes fastest.
Arguments:
- spectra: bfloat16 [2, 512, 16, 4096], P(None, 'sta', 'day')
- pair_stations: int32 [1280, 2], P('sta'), may hold values from 0 to 63
Outputs:
- stacked: float32 [1280, 4096], P(('sta', 'day'))
Inputs may be any that keep to these rules, and one draw needn't show every extreme that they name: `pair_stations`: in each round r of a block's rows, the first index names a station of the block and the second one of the block r below it, cyclically.
All inputs are finite; a program needn't handle non-finite values.
Results may differ from a plain program's by a relative error of at most 0.0034.
Values may be sent and summed in bfloat16 or wider, within the bound.
A program may use at most 256 MiB of HBM per device.

v0:
```python
import math

import jax
import jax.numpy as jnp
from jax import lax
from jax.sharding import PartitionSpec as P

LAGS = 4096


first_bin = 36
period = 72000
floor_value = 0.25


def from_behind(array, axis, by):
    devices = lax.axis_size(axis)
    return lax.ppermute(array, axis, [(i, (i + by) % devices) for i in range(devices)])


def band_taper(bin_count):
    position = lax.iota(jnp.int32, bin_count).astype(jnp.float32) + 0.5
    ramp = 8.0 / bin_count
    return jnp.minimum(1.0, jnp.minimum(position * ramp, (bin_count - position) * ramp))


def whiten(spectra):
    values = spectra.astype(jnp.float32)
    magnitude = jnp.sqrt(values[0] * values[0] + values[1] * values[1])
    return (values / jnp.maximum(magnitude, floor_value)[None]).astype(jnp.bfloat16)


def cross_spectra(left_rows, right_rows):
    left_re = left_rows[0].astype(jnp.float32)
    left_im = left_rows[1].astype(jnp.float32)
    right_re = right_rows[0].astype(jnp.float32)
    right_im = right_rows[1].astype(jnp.float32)
    taper = band_taper(left_rows.shape[-1])
    real_part = (left_re * right_re + left_im * right_im) * taper
    imag_part = (left_im * right_re - left_re * right_im) * taper
    return jnp.concatenate([real_part, imag_part], axis=-1).astype(jnp.bfloat16)


def lag_table(bin_count, lag_count, lag_start, lag_width):
    frequency = first_bin + lax.iota(jnp.int32, bin_count)
    lag_shift = lag_start + lax.iota(jnp.int32, lag_width) - lag_count // 2
    turns = jnp.remainder(frequency[:, None] * lag_shift[None, :], period).astype(jnp.float32)
    angle = turns * (2.0 * math.pi / period)
    cosine = jnp.cos(angle)
    sine = jnp.sin(angle)
    upper_half = jnp.concatenate([cosine, sine], axis=1)
    lower_half = jnp.concatenate([-sine, cosine], axis=1)
    return jnp.concatenate([upper_half, lower_half], axis=0).astype(jnp.bfloat16)


def analytic(cross_rows, lag_count):
    bin_count = cross_rows.shape[1] // 2
    lag_width = min(512, lag_count)
    real_blocks = []
    imag_blocks = []
    for block_number in range(lag_count // lag_width):
        table = lag_table(bin_count, lag_count, block_number * lag_width, lag_width)
        result = jnp.dot(cross_rows, table, preferred_element_type=jnp.float32) * (
            1.0 / math.sqrt(bin_count)
        )
        real_blocks.append(result[:, :lag_width])
        imag_blocks.append(result[:, lag_width:])
    return (jnp.concatenate(real_blocks, axis=1), jnp.concatenate(imag_blocks, axis=1))


def day_terms(cross, lag_count):
    row_count = cross.shape[0]
    day_number = cross.shape[1]
    real_part, imag_part = analytic(
        cross.reshape(row_count * day_number, cross.shape[2]), lag_count
    )
    real_part = real_part.reshape(row_count, day_number, lag_count)
    imag_part = imag_part.reshape(row_count, day_number, lag_count)
    magnitude = jnp.sqrt(real_part * real_part + imag_part * imag_part)
    denominator = jnp.maximum(magnitude, floor_value)
    return (
        jnp.sum(real_part, axis=1),
        jnp.sum(real_part / denominator, axis=1),
        jnp.sum(imag_part / denominator, axis=1),
    )


def phase_stack(real_sum, phase_re, phase_im, day_count):
    linear = real_sum / day_count
    coherent_re = phase_re / day_count
    coherent_im = phase_im / day_count
    return linear * (coherent_re * coherent_re + coherent_im * coherent_im)


def local(spectra, pair_stations):
    own_block = whiten(spectra)
    sta_count = lax.axis_size("sta")
    round_count = sta_count // 2 + 1
    pair_count = pair_stations.shape[0] // round_count
    lag_count = LAGS
    pieces = []
    for partner_round in range(round_count):
        if partner_round == 0:
            partner = own_block
        else:
            partner = from_behind(own_block, "sta", partner_round)
        rows_here = pair_stations[partner_round * pair_count : (partner_round + 1) * pair_count]
        left_rows = jnp.take(own_block, rows_here[:, 0], axis=1)
        right_rows = jnp.take(partner, rows_here[:, 1], axis=1)
        pieces.append(cross_spectra(left_rows, right_rows))
    cross = jnp.concatenate(pieces, axis=0)
    day_count = spectra.shape[2] * lax.axis_size("day")
    terms = day_terms(cross, lag_count)
    sums = jnp.stack([terms[0], terms[1], terms[2]], axis=0)
    mine = lax.psum_scatter(sums, "day", scatter_dimension=1, tiled=True)
    return phase_stack(mine[0], mine[1], mine[2], day_count)


def solution(mesh):
    placed = (P(None, "sta", "day", None), P("sta", None))
    return jax.shard_map(
        local, mesh=mesh, in_specs=placed, out_specs=P(("sta", "day"), None), check_vma=False
    )
```

profile of v0, /device:TPU:1, one launch (start us, length us, event | category | flops | bytes accessed | tf_op | source)
XLA Modules:
  0.0 787.6 jit_solution(10287180164766597415)
XLA Ops:
  6.5 2.4 copy_convert_fusion
  8.9 3.6 sqrt_maximum_fusion.1
  12.5 0.6 copy.67
  13.2 4.5 divide_convert_fusion
  17.7 4.4 collective-permute-start.3
  22.1 2.9 collective-permute-start
  25.0 0.5 collective-permute-start.2
  25.5 0.6 collective-permute-start.1
  26.1 3.7 fusion.241
  30.0 1.6 gather_fusion
  31.7 1.6 gather_fusion.1
  33.3 1.2 bitcast_select_fusion.8
  34.5 0.9 fusion.228
  35.4 289.1 %fusion.83 = (bf16[4096,512]{1,0:T(8,128)(2,1)}, bf16[4096,512]{1,0:T(8,128)(2,1)}, bf16[4096,512]{1,0:T(8,128)(2,1)}, bf16[4096,512]{1,0:T(8,128)(2,1)}, bf16[4...) fusion(s32[512]{0:T(512)S(1)} %get-tuple-element.118, ...), kind=kLoop, calls=%fused_computation.104 | loop fusion | flops 218103808 | bytes 100694016 | tf_op jit(solution)/shard_map/convert.5
  324.6 1.6 gather_fusion.8
  326.2 1.6 gather_fusion.2
  327.8 1.6 gather_fusion.6
  329.4 1.6 gather_fusion.4
  331.0 1.8 maximum_dynamic-update-slice_fusion.4
  332.9 3.6 gather_fusion.9
  336.4 3.6 gather_fusion.3
  340.0 2.8 gather_fusion.7
  342.9 2.8 gather_fusion.5
  345.7 2.4 bitcast_select_fusion
  348.1 2.3 bitcast_select_fusion.6
  350.4 0.7 fusion.220
  351.1 1.2 bitcast_select_fusion.2
  352.3 1.2 bitcast_select_fusion.4
  353.6 0.4 fusion.222
  354.2 1.5 copy-done.10
  355.6 17.7 %fusion.165 = f32[160,1024]{1,0:T(8,128)S(1)} fusion(bf16[4096,512]{1,0:T(8,128)(2,1)} %get-tuple-element.75, bf16[4096,512]{1,0:T(8,128)(2,1)} %get-tuple-element.76, bf16[4096,512]{1,0:T(8,128)(2,1)} %get-tuple-element.77, bf16[160,1,8192]{2,0,1:T(8,128)(2,1)} %copy-done.10), kind=kOutput, calls=%fused_computation.182 | convolution fusion | flops 2751627264 | bytes 15859712 | tf_op jit(solution)/shard_map/dot_general | solution.py:63
  373.3 0.8 slice_dynamic-update-slice_fusion.7
  374.1 0.8 bitcast_dynamic-update-slice_fusion.7
  374.9 17.7 %fusion.160 = f32[160,1024]{1,0:T(8,128)S(1)} fusion(bf16[4096,512]{1,0:T(8,128)(2,1)} %get-tuple-element.81, bf16[4096,512]{1,0:T(8,128)(2,1)} %get-tuple-element.82, bf16[4096,512]{1,0:T(8,128)(2,1)} %get-tuple-element.83, bf16[160,1,8192]{2,0,1:T(8,128)(2,1)} %copy-done.10), kind=kOutput, calls=%fused_computation.181 | convolution fusion | flops 2751627264 | bytes 15859712 | tf_op jit(solution)/shard_map/dot_general | solution.py:63
  392.6 0.8 slice_dynamic-update-slice_fusion.6
  393.5 19.4 %fusion.155 = f32[160,1024]{1,0:T(8,128)} fusion(bf16[4096,512]{1,0:T(8,128)(2,1)} %get-tuple-element.93, bf16[4096,512]{1,0:T(8,128)(2,1)} %get-tuple-element.94, bf16[4096,512]{1,0:T(8,128)(2,1)} %get-tuple-element.95, bf16[160,1,8192]{2,0,1:T(8,128)(2,1)} %copy-done.10), kind=kOutput, calls=%fused_computation.180 | convolution fusion | flops 2751627264 | bytes 15859712 | tf_op jit(solution)/shard_map/dot_general | solution.py:63
  412.8 1.8 slice_dynamic-update-slice_fusion.5
  414.6 17.7 %fusion.150 = f32[160,1024]{1,0:T(8,128)S(1)} fusion(bf16[4096,512]{1,0:T(8,128)(2,1)} %get-tuple-element.90, bf16[4096,512]{1,0:T(8,128)(2,1)} %get-tuple-element.91, bf16[4096,512]{1,0:T(8,128)(2,1)} %get-tuple-element.92, bf16[160,1,8192]{2,0,1:T(8,128)(2,1)} %copy-done.10), kind=kOutput, calls=%fused_computation.179 | convolution fusion | flops 2751627264 | bytes 15859712 | tf_op jit(solution)/shard_map/dot_general | solution.py:63
  432.3 0.9 slice_dynamic-update-slice_fusion.4
  433.2 17.9 %fusion.145 = f32[160,1024]{1,0:T(8,128)S(1)} fusion(bf16[4096,512]{1,0:T(8,128)(2,1)} %get-tuple-element.87, bf16[4096,512]{1,0:T(8,128)(2,1)} %get-tuple-element.89, bf16[4096,512]{1,0:T(8,128)(2,1)} %get-tuple-element.88, bf16[160,1,8192]{2,0,1:T(8,128)(2,1)} %copy-done.10), kind=kOutput, calls=%fused_computation.178 | convolution fusion | flops 2751627264 | bytes 15859712 | tf_op jit(solution)/shard_map/dot_general | solution.py:63
  451.1 0.9 slice_dynamic-update-slice_fusion.3
  452.0 0.1 copy-done.5
  452.1 17.7 %fusion.140 = f32[160,1024]{1,0:T(8,128)S(1)} fusion(bf16[4096,512]{1,0:T(8,128)(2,1)} %get-tuple-element.84, bf16[4096,512]{1,0:T(8,128)(2,1)} %get-tuple-element.85, bf16[4096,512]{1,0:T(8,128)(2,1)} %get-tuple-element.86, bf16[160,1,8192]{2,0,1:T(8,128)(2,1)} %copy-done.10), kind=kOutput, calls=%fused_computation.177 | convolution fusion | flops 2751627264 | bytes 15859712 | tf_op jit(solution)/shard_map/dot_general | solution.py:63
  469.8 0.8 slice_dynamic-update-slice_fusion.2
  470.6 0.1 copy-done.3
  470.8 17.7 %fusion.135 = f32[160,1024]{1,0:T(8,128)S(1)} fusion(bf16[4096,512]{1,0:T(8,128)(2,1)} %get-tuple-element.78, bf16[4096,512]{1,0:T(8,128)(2,1)} %get-tuple-element.79, bf16[4096,512]{1,0:T(8,128)(2,1)} %get-tuple-element.80, bf16[160,1,8192]{2,0,1:T(8,128)(2,1)} %copy-done.10), kind=kOutput, calls=%fused_computation.176 | convolution fusion | flops 2751627264 | bytes 15859712 | tf_op jit(solution)/shard_map/dot_general | solution.py:63
  488.5 0.8 slice_dynamic-update-slice_fusion.1
  489.2 19.2 %fusion.130 = f32[160,1024]{1,0:T(8,128)} fusion(bf16[4096,512]{1,0:T(8,128)(2,1)} %get-tuple-element.56, bf16[4096,512]{1,0:T(8,128)(2,1)} %get-tuple-element.55, bf16[4096,512]{1,0:T(8,128)(2,1)} %get-tuple-element.54, bf16[160,1,8192]{2,0,1:T(8,128)(2,1)} %copy-done.10), kind=kOutput, calls=%fused_computation.175 | convolution fusion | flops 2751627264 | bytes 15859712 | tf_op jit(solution)/shard_map/dot_general | solution.py:63
  508.4 1.9 slice_dynamic-update-slice_fusion
  510.3 1.9 bitcast_dynamic-update-slice_fusion.6
  512.2 1.9 bitcast_dynamic-update-slice_fusion.5
  514.0 1.9 bitcast_dynamic-update-slice_fusion.4
  515.9 0.8 bitcast_dynamic-update-slice_fusion.3
  516.7 0.8 bitcast_dynamic-update-slice_fusion.2
  517.5 0.8 bitcast_dynamic-update-slice_fusion.1
  518.3 0.8 bitcast_dynamic-update-slice_fusion
  519.1 3.1 fusion.129
  522.2 3.8 pad_maximum_fusion
  526.0 12.7 %copy.47 = f32[3,160,4096]{2,0,1:T(4,128)} copy(f32[3,160,4096]{2,1,0:T(8,128)} %pad_maximum_fusion) | data formatting | bytes 15728640 | tf_op jit(solution)/shard_map/stack | solution.py:114
  538.7 0.6 copy-done.12
  539.3 0.6 dynamic-slice
  540.6 237.1 %all-reduce.3.cloned.1.call-done = f32[3,160,4096]{2,0,1:T(4,128)} async-done(((f32[3,160,4096]{2,0,1:T(4,128)}), f32[3,160,4096]{2,0,1:T(4,128)}) %all-reduce.3.cloned.1.call-update) | async-done | bytes 7864336
  777.7 2.0 fusion.232
  779.7 0.8 copy.68
  (49 shorter events, 0.5 us)
Async XLA Ops:
  6.5 6.6 copy-start
  6.5 771.2 %all-reduce.3.cloned.1.call-start = ((), (), s32[]{:S(2)}) async-start(), calls=%async_computation | async-start | bytes 20971520
  12.5 17.4 %copy-start.11 = (s32[160,2]{0,1:T(2,128)S(1)}, s32[160,2]{0,1:T(2,128)}, u32[]{:S(2)}) copy-start(s32[160,2]{0,1:T(2,128)} %param.5) | copy-start | bytes 3844
  17.7 315.2 %collective-permute-start.3 = (bf16[2,64,1,4096]{3,0,1,2:T(2,128)(2,1)}, bf16[2,64,1,4096]{3,0,1,2:T(2,128)(2,1)}, u32[]{:S(2)}, u32[]{:S(2)}) collective-permute-start(bf16[2,64,1,4096]{3,0,1,2:T(2,128)(2,1)} %divide_convert_fusion), channel_id=1, source_target_pairs={{0,64},{16,80},{32,96},{48,112},{64,0},{80,16},{96,32},{112,48},{1... | collective-permute-start | bytes 3145736 | tf_op jit(solution)/shard_map/ppermute | solution.py:18
  22.1 314.4 %collective-permute-start = (bf16[2,64,1,4096]{3,0,1,2:T(2,128)(2,1)}, bf16[2,64,1,4096]{3,0,1,2:T(2,128)(2,1)}, u32[]{:S(2)}, u32[]{:S(2)}) collective-permute-start(bf16[2,64,1,4096]{3,0,1,2:T(2,128)(2,1)} %divide_convert_fusion), channel_id=1, source_target_pairs={{0,16},{16,32},{32,48},{48,64},{64,80},{80,96},{96,112},{112,0},{1... | collective-permute-start | bytes 3145736 | tf_op jit(solution)/shard_map/ppermute | solution.py:18
  25.0 315.0 %collective-permute-start.2 = (bf16[2,64,1,4096]{3,0,1,2:T(2,128)(2,1)}, bf16[2,64,1,4096]{3,0,1,2:T(2,128)(2,1)}, u32[]{:S(2)}, u32[]{:S(2)}) collective-permute-start(bf16[2,64,1,4096]{3,0,1,2:T(2,128)(2,1)} %divide_convert_fusion), channel_id=1, source_target_pairs={{0,48},{16,64},{32,80},{48,96},{64,112},{80,0},{96,16},{112,32},{1... | collective-permute-start | bytes 3145736 | tf_op jit(solution)/shard_map/ppermute | solution.py:18
  25.5 317.4 %collective-permute-start.1 = (bf16[2,64,1,4096]{3,0,1,2:T(2,128)(2,1)}, bf16[2,64,1,4096]{3,0,1,2:T(2,128)(2,1)}, u32[]{:S(2)}, u32[]{:S(2)}) collective-permute-start(bf16[2,64,1,4096]{3,0,1,2:T(2,128)(2,1)} %divide_convert_fusion), channel_id=1, source_target_pairs={{0,32},{16,48},{32,64},{48,80},{64,96},{80,112},{96,0},{112,16},{1... | collective-permute-start | bytes 3145736 | tf_op jit(solution)/shard_map/ppermute | solution.py:18
  345.7 5.4 copy-start.9
  354.2 1.5 copy-start.10
  392.6 20.2 %copy-start.7 = (f32[160,1024]{1,0:T(8,128)}, f32[160,1024]{1,0:T(8,128)S(1)}, u32[]{:S(2)}) copy-start(f32[160,1024]{1,0:T(8,128)S(1)} %fusion.160) | copy-start | bytes 1966084
  432.3 1.0 copy-start.8
  451.1 1.0 copy-start.5
  469.8 1.0 copy-start.3
  508.4 7.5 copy-start.6
  508.4 8.3 %copy-start.4 = (f32[160,1024]{1,0:T(8,128)S(1)}, f32[160,1024]{1,0:T(8,128)}, u32[]{:S(2)}) copy-start(f32[160,1024]{1,0:T(8,128)} %copy-done.3) | copy-start | bytes 1966084
  508.4 9.9 %copy-start.2 = (f32[160,1024]{1,0:T(8,128)S(1)}, f32[160,1024]{1,0:T(8,128)}, u32[]{:S(2)}) copy-start(f32[160,1024]{1,0:T(8,128)} %fusion.130) | copy-start | bytes 1966084
  519.1 3.1 copy-start.1
  538.7 0.7 copy-start.12
Sparse Core Ops, SparseCore 0:
  538.8 238.8 all-reduce.2
where the time goes:
time: 794 us; the launch traced here: 788 us
  other arithmetic  325 us (41%)
  waiting for transfers between devices  237 us (30%)
  matrix products  145 us (18%)
  local copies, waits for them, and re-layouts  57.8 us (7%)
  between operations  14.8 us (2%)
  starting transfers between devices  8.4 us (1%)
    another operation x1, other arithmetic  289 us
    unnamed x2, waiting for transfers between devices  237 us
    dot_general x8, matrix products, analytic(): jnp.dot(cross_rows, table, preferred_element_type=jnp.float32)  145 us
    unnamed x43, local copies, waits for them, and re-layouts  20 us
  transfers between devices with their start and end apart: 5, of which 1 were waited for; matrix products, arithmetic and copies ran while one was open for 40% of the time, Pallas kernels for 0%

commit v1 on v0

v1 whole, which is shorter than its diff:
```python
import functools
import math

import numpy as np
import jax
import jax.numpy as jnp
import ml_dtypes
from jax import lax
from jax.experimental import pallas as pl
from jax.experimental.pallas import tpu as pltpu
from jax.sharding import PartitionSpec as P

BINS = 4096
LAGS = 4096
STA = 8
DAY = 16
STATIONS = 64
ROUNDS = 5
PAIRS = 32
ROWS = ROUNDS * PAIRS
MINE = ROWS // DAY
WIDTH = BINS // STA
RANK = 64
SLOT = 16
LAG_TILE = 512
TILES = LAGS // LAG_TILE
FIRST_BIN = 36
PERIOD = 72000
MESH = pl.DeviceIdType.MESH
F32 = jnp.float32
BF16 = jnp.bfloat16


def prolate_basis(width, rank):
    t = np.arange(width, dtype=np.float64)
    half_band = LAGS / 2 / PERIOD
    diagonal = ((width - 1 - 2 * t) / 2) ** 2 * np.cos(2 * np.pi * half_band)
    off = t[1:] * (width - t[1:]) / 2
    matrix = np.diag(diagonal) + np.diag(off, 1) + np.diag(off, -1)
    _, vectors = np.linalg.eigh(matrix)
    vectors = vectors[:, ::-1][:, :rank]
    middle = width // 2
    signs = np.sign(vectors[middle])
    return vectors * signs[None]


@functools.lru_cache(maxsize=None)
def tables():
    basis = prolate_basis(WIDTH, RANK)
    lag = np.arange(LAGS, dtype=np.int64) - LAGS // 2
    rows = []
    for block in range(STA):
        bins = FIRST_BIN + block * WIDTH + np.arange(WIDTH, dtype=np.int64)
        turns = np.remainder(bins[:, None] * lag[None, :], PERIOD)
        angle = turns * (2.0 * np.pi / PERIOD)
        cosine, sine = np.cos(angle), np.sin(angle)
        rows.append(basis.T @ cosine)
        rows.append(-(basis.T @ sine))
    table = np.concatenate(rows, axis=0) / math.sqrt(BINS)
    table = table.reshape(STA * 2 * RANK, TILES, LAG_TILE).transpose(1, 0, 2)
    forward = np.zeros((2 * WIDTH, 2 * RANK))
    forward[:WIDTH, :RANK] = basis
    forward[WIDTH:, RANK:] = basis
    spread = np.zeros((DAY * SLOT, ROWS))
    for row in range(ROWS):
        spread[row // MINE * SLOT + row % MINE, row] = 1.0
    turn = np.zeros((2 * RANK, 2 * RANK))
    for i in range(RANK):
        turn[RANK + i, i] = 1.0
        turn[i, RANK + i] = -1.0
    as_bf16 = lambda a: np.ascontiguousarray(a).astype(ml_dtypes.bfloat16)
    return as_bf16(table), as_bf16(forward), as_bf16(spread), as_bf16(turn)


def dot(a, b):
    return jnp.dot(a, b, preferred_element_type=F32)


def exchange_bins(x_ref, idx_ref, w_ref, i_ref, send, isend, wsem, wrsem, isem, irsem):
    me = lax.axis_index("sta")
    barrier = pltpu.get_barrier_semaphore()
    for step in range(1, STA):
        pl.semaphore_signal(barrier, inc=1, device_id={"sta": lax.rem(me + step, STA)}, device_id_type=MESH)
    isend[...] = jnp.zeros_like(isend)
    isend[0:2, 0:ROWS] = idx_ref[...]
    for part in range(STA):
        re = x_ref[0, :, part * WIDTH : (part + 1) * WIDTH].astype(F32)
        im = x_ref[1, :, part * WIDTH : (part + 1) * WIDTH].astype(F32)
        scale = jnp.minimum(lax.rsqrt(re * re + im * im), 4.0)
        send[part, :, 0:WIDTH] = (re * scale).astype(BF16)
        send[part, :, WIDTH:] = (im * scale).astype(BF16)
    pl.semaphore_wait(barrier, STA - 1)
    copies = []
    for step in (4, 3, 5, 2, 6, 1, 7):
        to = lax.rem(me + step, STA)
        copies.append(
            pltpu.make_async_remote_copy(
                src_ref=isend, dst_ref=i_ref.at[me], send_sem=isem.at[step], recv_sem=irsem.at[step],
                device_id={"sta": to}, device_id_type=MESH,
            )
        )
        copies.append(
            pltpu.make_async_remote_copy(
                src_ref=send.at[to], dst_ref=w_ref.at[me], send_sem=wsem.at[step], recv_sem=wrsem.at[step],
                device_id={"sta": to}, device_id_type=MESH,
            )
        )
    for copy in copies:
        copy.start()
    w_ref[me] = send[me]
    i_ref[me] = isend[...]
    for copy in copies:
        copy.wait()


def coefficients(me_ref, w_ref, i_ref, forward_ref, spread_ref, y_ref, u_buf, v_buf):
    me = me_ref[0]
    lanes = lax.broadcasted_iota(jnp.int32, (ROWS, STATIONS), 1)

    def pick(block, _):
        first = jnp.transpose(i_ref[block])[0:ROWS, 0:1]
        seconds = []
        for r in range(ROUNDS):
            other = lax.rem(block + r, STA)
            seconds.append(jnp.transpose(i_ref[other])[r * PAIRS : (r + 1) * PAIRS, 1:2])
        second = jnp.concatenate(seconds, axis=0)
        hot = jnp.concatenate([first == lanes, second == lanes], axis=0)
        hot = jnp.where(hot, 1.0, 0.0).astype(BF16)
        got = dot(hot, w_ref[block]).astype(BF16)
        u_buf[block] = got[0:ROWS]
        for r in range(ROUNDS):
            v_buf[lax.rem(block + r, STA), r * PAIRS : (r + 1) * PAIRS, :] = got[ROWS + r * PAIRS : ROWS + (r + 1) * PAIRS]
        return 0

    lax.fori_loop(0, STA, pick, 0)
    position = (lax.broadcasted_iota(jnp.int32, (1, WIDTH), 1) + me * WIDTH).astype(F32) + 0.5
    ramp = 8.0 / BINS
    taper = jnp.minimum(1.0, jnp.minimum(position * ramp, (BINS - position) * ramp))

    def cross(block, _):
        ur = u_buf[block, :, 0:WIDTH].astype(F32)
        ui = u_buf[block, :, WIDTH:].astype(F32)
        vr = v_buf[block, :, 0:WIDTH].astype(F32)
        vi = v_buf[block, :, WIDTH:].astype(F32)
        cr = ((ur * vr + ui * vi) * taper).astype(BF16)
        ci = ((ui * vr - ur * vi) * taper).astype(BF16)
        y = dot(cr, forward_ref[0:WIDTH]) + dot(ci, forward_ref[WIDTH:])
        y_ref[block] = dot(spread_ref[...], y.astype(BF16)).astype(BF16)
        return 0

    lax.fori_loop(0, STA, cross, 0)


def exchange_rows(y_ref, z_ref, ssem, rsem):
    s = lax.axis_index("sta")
    d = lax.axis_index("day")
    me = s * DAY + d
    barrier = pltpu.get_barrier_semaphore()
    count = STA * DAY

    def greet(step, _):
        to = lax.rem(me + step, count)
        pl.semaphore_signal(barrier, inc=1, device_id=(to // DAY, lax.rem(to, DAY)), device_id_type=MESH)
        return 0

    lax.fori_loop(1, count, greet, 0)
    pl.semaphore_wait(barrier, count - 1)

    def push(step, _):
        to = lax.rem(me + step, count)
        pltpu.make_async_remote_copy(
            src_ref=y_ref.at[to], dst_ref=z_ref.at[me], send_sem=ssem, recv_sem=rsem,
            device_id=(to // DAY, lax.rem(to, DAY)), device_id_type=MESH,
        ).start()
        return 0

    lax.fori_loop(1, count, push, 0)
    z_ref[me] = y_ref[me]
    rest = z_ref.at[pl.ds(0, count - 1)]
    pltpu.make_async_copy(rest, rest, ssem).wait()
    pltpu.make_async_copy(rest, rest, rsem).wait()


def stack_days(z_ref, table_ref, spread_ref, turn_ref, out_ref, left, sums):
    for s in range(STA):
        rows = z_ref[s * DAY : (s + 1) * DAY].reshape(DAY * SLOT, 2 * RANK)
        packed = lax.dot_general(spread_ref[...], rows, (((0,), (0,)), ((), ())), preferred_element_type=F32).astype(BF16)
        left[0:ROWS, s * 2 * RANK : (s + 1) * 2 * RANK] = packed
        left[ROWS:, s * 2 * RANK : (s + 1) * 2 * RANK] = dot(packed, turn_ref[...]).astype(BF16)
    group = 4 * MINE

    def tile(t, _):
        both = dot(left[...], table_ref[t])
        re, im = both[0:ROWS], both[ROWS:]
        scale = jnp.minimum(lax.rsqrt(re * re + im * im), 4.0)
        parts = (re, re * scale, im * scale)
        for n, part in enumerate(parts):
            total = part[0:group]
            for g in range(1, ROWS // group):
                total = total + part[g * group : (g + 1) * group]
            sums[n] = total
        done = []
        for n in range(3):
            total = sums[n, 0:MINE, :]
            for g in range(1, 4):
                total = total + sums[n, g * MINE : (g + 1) * MINE, :]
            done.append(total * (1.0 / DAY))
        out_ref[:, pl.ds(pl.multiple_of(t * LAG_TILE, LAG_TILE), LAG_TILE)] = done[0] * (done[1] * done[1] + done[2] * done[2])
        return 0

    lax.fori_loop(0, TILES, tile, 0)


def local(spectra, pair_stations):
    table, forward, spread, turn = (jnp.asarray(a) for a in tables())
    vmem = pl.BlockSpec(memory_space=pltpu.VMEM)
    smem = pl.BlockSpec(memory_space=pltpu.SMEM)
    limit = 56 << 20
    x = spectra.reshape(2, STATIONS, BINS)
    idx = pair_stations.T
    w, i = pl.pallas_call(
        exchange_bins,
        name="exchange_bins",
        out_shape=(jax.ShapeDtypeStruct((STA, STATIONS, 2 * WIDTH), BF16), jax.ShapeDtypeStruct((STA, 8, 256), jnp.int32)),
        in_specs=[vmem, vmem],
        out_specs=(vmem, vmem),
        scratch_shapes=[
            pltpu.VMEM((STA, STATIONS, 2 * WIDTH), BF16),
            pltpu.VMEM((8, 256), jnp.int32),
            pltpu.SemaphoreType.DMA((STA,)),
            pltpu.SemaphoreType.DMA((STA,)),
            pltpu.SemaphoreType.DMA((STA,)),
            pltpu.SemaphoreType.DMA((STA,)),
        ],
        compiler_params=pltpu.CompilerParams(collective_id=0, has_side_effects=True, vmem_limit_bytes=limit),
    )(x, idx)
    me = lax.axis_index("sta").astype(jnp.int32).reshape(1)
    y = pl.pallas_call(
        coefficients,
        name="coefficients",
        out_shape=jax.ShapeDtypeStruct((STA, DAY * SLOT, 2 * RANK), BF16),
        in_specs=[smem, vmem, vmem, vmem, vmem],
        out_specs=vmem,
        scratch_shapes=[pltpu.VMEM((STA, ROWS, 2 * WIDTH), BF16)] * 2,
        compiler_params=pltpu.CompilerParams(vmem_limit_bytes=limit),
    )(me, w, i, forward, spread)
    z = pl.pallas_call(
        exchange_rows,
        name="exchange_rows",
        out_shape=jax.ShapeDtypeStruct((STA * DAY, SLOT, 2 * RANK), BF16),
        in_specs=[vmem],
        out_specs=vmem,
        scratch_shapes=[pltpu.SemaphoreType.DMA, pltpu.SemaphoreType.DMA],
        compiler_params=pltpu.CompilerParams(collective_id=1, has_side_effects=True, vmem_limit_bytes=limit),
    )(y.reshape(STA * DAY, SLOT, 2 * RANK))
    return pl.pallas_call(
        stack_days,
        name="stack_days",
        out_shape=jax.ShapeDtypeStruct((MINE, LAGS), F32),
        in_specs=[vmem] * 4,
        out_specs=vmem,
        scratch_shapes=[pltpu.VMEM((2 * ROWS, STA * 2 * RANK), BF16), pltpu.VMEM((3, 4 * MINE, LAG_TILE), F32)],
        compiler_params=pltpu.CompilerParams(vmem_limit_bytes=limit),
    )(z, table, spread, turn)


def solution(mesh):
    placed = (P(None, "sta", "day", None), P("sta", None))
    return jax.shard_map(
        local, mesh=mesh, in_specs=placed, out_specs=P(("sta", "day"), None), check_vma=False
    )
```

time: 794 us -> 63.8 us (0.08)
  other arithmetic: 325 us -> 0 us
  waiting for transfers between devices: 237 us -> 0 us
  matrix products: 145 us -> 0 us
  Pallas kernels: 0 us -> 63.6 us
  local copies, waits for them, and re-layouts: 57.8 us -> 0 us
  between operations: 14.8 us -> 0.02 us
  starting transfers between devices: 8.4 us -> 0 us
    another operation x3 -> x0, other arithmetic: 297 us -> none
    unnamed x2 -> x0, waiting for transfers between devices: 237 us -> none
    dot_general x8 -> x0, matrix products: 145 us -> none  [analytic(): jnp.dot(cross_rows, table, preferred_element_type=jnp.float32)]
    pallas_call x0 -> x4, Pallas kernels: none -> 63.6 us  [the longest x1 23.5 us: local(): pl.pallas_call(exchange_bins, name='exchange_bins', out_shape=(jax.ShapeD...]
    gather x10 -> x0, local copies, waits for them, and re-layouts: 22.4 us -> none  [the longest x5 14.4 us: local(): right_rows = jnp.take(partner, rows_here[:, 1], axis=1)]
    unnamed x43 -> x0, local copies, waits for them, and re-layouts: 20 us -> none
    another operation x1 -> x0, local copies, waits for them, and re-layouts: 12.7 us -> none  [local(): sums = jnp.stack([terms[0], terms[1], terms[2]], axis=0)]
    ppermute x4 -> x0, starting transfers between devices: 8.39 us -> none  [from_behind(): lax.ppermute(array, axis, [(i, (i + by) % devices) for i in range(devices)])]
  transfers between devices with their start and end apart: 5 -> 0, of which waited for: 1 -> 0; matrix products, arithmetic and copies ran while one was open for 40% -> 0% of each run, Pallas kernels for 0% -> 0%
where the time goes in v1:
time: 63.8 us; the launch traced here: 63.6 us
  Pallas kernels  63.6 us (100%)
    pallas_call x1, Pallas kernels, local(): pl.pallas_call(exchange_bins, name='exchange_bins', out_shape=(jax.ShapeD...  23.5 us
    pallas_call x1, Pallas kernels, local(): pl.pallas_call(exchange_rows, name='exchange_rows', out_shape=jax.ShapeDt...  18.8 us
    pallas_call x1, Pallas kernels, local(): pl.pallas_call(coefficients, name='coefficients', out_shape=jax.ShapeDtyp...  10.9 us
    pallas_call x1, Pallas kernels, local(): pl.pallas_call(stack_days, name='stack_days', out_shape=jax.ShapeDtypeStr...  10.5 us

profile of v1, /device:TPU:1, one launch (start us, length us, event | category | flops | bytes accessed | tf_op | source)
XLA Modules:
  0.0 63.6 jit_solution(3071350060080626754)
XLA Ops:
  0.0 23.5 %exchange_bins.1 = (bf16[8,64,1024]{2,1,0:T(8,128)(2,1)}, s32[8,8,256]{2,1,0:T(8,128)}) custom-call(bf16[2,64,4096]{2,1,0:T(8,128)(2,1)} %bitcast.5, s32[2,160]{1,0:T(2,128)} %bitcast.6), custom_call_target="tpu_custom_call" | custom-call | tf_op jit(solution)/shard_map/exchange_bins/pallas_call | solution.py:221
  23.5 10.9 %coefficients.1 = bf16[8,256,128]{2,1,0:T(8,128)(2,1)} custom-call(s32[1]{0:T(128)} %bitcast.me_ref, bf16[8,64,1024]{2,1,0:T(8,128)(2,1)} %get-tuple-element.7.w_ref, s32[8,8,256]{2,1,0:T(8,128)} %get-tuple-element.8.i_ref, bf16[1024,128]{1,0:T(8,128)(2,1)} %constant.15.clone.forward_ref, bf16[256,160]{1,0:T(8,128)(2,1)} %constant.16.clone.spread_ref), custom_call_target="tpu_custom_call" | custom-call | tf_op jit(solution)/shard_map/coefficients/pallas_call | solution.py:238
  34.3 18.8 %exchange_rows.1.z_ref = bf16[128,16,128]{2,1,0:T(8,128)(2,1)} custom-call(bf16[128,16,128]{2,1,0:T(8,128)(2,1)} %bitcast.4), custom_call_target="tpu_custom_call" | custom-call | tf_op jit(solution)/shard_map/exchange_rows/pallas_call | solution.py:247
  53.1 10.5 %stack_days.1 = f32[10,4096]{1,0:T(8,128)} custom-call(bf16[128,16,128]{2,1,0:T(8,128)(2,1)} %exchange_rows.1.z_ref, bf16[8,1024,512]{2,1,0:T(8,128)(2,1)} %constant.14.clone.table_ref, bf16[256,160]{1,0:T(8,128)(2,1)} %constant.16.clone.spread_ref, bf16[128,128]{1,0:T(8,128)(2,1)} %constant.17.clone.turn_ref), custom_call_target="tpu_custom_call" | custom-call | tf_op jit(solution)/shard_map/stack_days/pallas_call | solution.py:256

commit v2 on v1

v2 whole, which is shorter than its diff:
```python
import functools
import math

import numpy as np
import jax
import jax.numpy as jnp
import ml_dtypes
from jax import lax
from jax.experimental import pallas as pl
from jax.experimental.pallas import tpu as pltpu
from jax.sharding import PartitionSpec as P

BINS = 4096
LAGS = 4096
STA = 8
DAY = 16
STATIONS = 64
ROUNDS = 5
PAIRS = 32
ROWS = ROUNDS * PAIRS
MINE = ROWS // DAY
WIDTH = BINS // STA
RANK = 64
SLOT = 16
LAG_TILE = 512
TILES = LAGS // LAG_TILE
HALVES = 2
HALF = WIDTH // HALVES
DEVICES = STA * DAY
ORDER = (4, 3, 5, 2, 6, 1, 7)
FIRST_BIN = 36
PERIOD = 72000
MESH = pl.DeviceIdType.MESH
F32 = jnp.float32
BF16 = jnp.bfloat16


def prolate_basis(width, rank):
    t = np.arange(width, dtype=np.float64)
    half_band = LAGS / 2 / PERIOD
    diagonal = ((width - 1 - 2 * t) / 2) ** 2 * np.cos(2 * np.pi * half_band)
    off = t[1:] * (width - t[1:]) / 2
    matrix = np.diag(diagonal) + np.diag(off, 1) + np.diag(off, -1)
    _, vectors = np.linalg.eigh(matrix)
    vectors = vectors[:, ::-1][:, :rank]
    middle = width // 2
    signs = np.sign(vectors[middle])
    return vectors * signs[None]


@functools.lru_cache(maxsize=None)
def tables():
    basis = prolate_basis(WIDTH, RANK)
    lag = np.arange(LAGS, dtype=np.int64) - LAGS // 2
    rows = []
    for block in range(STA):
        bins = FIRST_BIN + block * WIDTH + np.arange(WIDTH, dtype=np.int64)
        turns = np.remainder(bins[:, None] * lag[None, :], PERIOD)
        angle = turns * (2.0 * np.pi / PERIOD)
        cosine, sine = np.cos(angle), np.sin(angle)
        rows.append(basis.T @ cosine)
        rows.append(-(basis.T @ sine))
    table = np.concatenate(rows, axis=0) / math.sqrt(BINS)
    table = table.reshape(STA * 2 * RANK, TILES, LAG_TILE).transpose(1, 0, 2)
    high = basis.astype(ml_dtypes.bfloat16).astype(np.float64)
    forward = np.zeros((HALVES, 2, HALF, 4, RANK))
    for half in range(HALVES):
        rows = slice(half * HALF, (half + 1) * HALF)
        for n, part in enumerate((high, basis - high)):
            forward[half, 0, :, 2 * n] = part[rows]
            forward[half, 1, :, 2 * n + 1] = part[rows]
    forward = forward.reshape(HALVES, 2 * HALF, 4 * RANK)
    spread = np.zeros((DAY * SLOT, ROWS))
    for row in range(ROWS):
        spread[row // MINE * SLOT + row % MINE, row] = 1.0
    as_bf16 = lambda a: np.ascontiguousarray(a).astype(ml_dtypes.bfloat16)
    return as_bf16(table), as_bf16(forward), as_bf16(spread)


def dot(a, b):
    return jnp.dot(a, b, preferred_element_type=F32)


def correlate(x_ref, idx_ref, forward_ref, spread_ref, table_hbm, out_ref,
              send, recv, isend, irecv, hot, u_buf, v_buf, y_sum, y_buf, z_buf, left, sums, table,
              wsem, wrsem, isem, irsem, tsem, ssem, rsem):
    s = lax.axis_index("sta")
    d = lax.axis_index("day")
    me = s * DAY + d

    barrier = pltpu.get_barrier_semaphore()
    for step in range(1, STA):
        pl.semaphore_signal(barrier, inc=1, device_id=(lax.rem(s + step, STA), d), device_id_type=MESH)
    for step in range(1, DAY):
        pl.semaphore_signal(barrier, inc=1, device_id=(s, lax.rem(d + step, DAY)), device_id_type=MESH)

    def whiten(half):
        for part in range(STA):
            at = part * WIDTH + half * HALF
            re = x_ref[0, :, at : at + HALF].astype(F32)
            im = x_ref[1, :, at : at + HALF].astype(F32)
            scale = jnp.minimum(lax.rsqrt(re * re + im * im), 4.0)
            send[half, part, :, 0:HALF] = (re * scale).astype(BF16)
            send[half, part, :, HALF:] = (im * scale).astype(BF16)

    def bins_copy(half, step):
        to = lax.rem(s + step, STA)
        return pltpu.make_async_remote_copy(
            src_ref=send.at[half, to], dst_ref=recv.at[half, s],
            send_sem=wsem.at[half, step], recv_sem=wrsem.at[half, step],
            device_id=(to, d), device_id_type=MESH,
        )

    def pairs_copy(step):
        return pltpu.make_async_remote_copy(
            src_ref=isend, dst_ref=irecv.at[s], send_sem=isem.at[step], recv_sem=irsem.at[step],
            device_id=(lax.rem(s + step, STA), d), device_id_type=MESH,
        )

    def table_copy(t):
        return pltpu.make_async_copy(table_hbm.at[t], table.at[t], tsem.at[t])

    isend[...] = jnp.zeros_like(isend)
    isend[0:2, 0:ROWS] = idx_ref[...]
    whiten(0)
    pl.semaphore_wait(barrier, STA + DAY - 2)
    for step in ORDER:
        pairs_copy(step).start()
    for step in ORDER:
        bins_copy(0, step).start()
    for half in range(1, HALVES):
        whiten(half)
        for step in ORDER:
            bins_copy(half, step).start()
    for t in range(TILES):
        table_copy(t).start()
    for half in range(HALVES):
        recv[half, s] = send[half, s]
    irecv[s] = isend[...]

    for step in ORDER:
        pairs_copy(step).wait()
    lanes = lax.broadcasted_iota(jnp.int32, (ROWS, STATIONS), 1)

    def choose(block, _):
        rows = jnp.transpose(irecv[block])
        hot[block, 0:ROWS] = jnp.where(rows[0:ROWS, 0:1] == lanes, 1.0, 0.0).astype(BF16)
        second = jnp.where(rows[0:ROWS, 1:2] == lanes, 1.0, 0.0).astype(BF16)
        for r in range(ROUNDS):
            partner = lax.rem(block - r + STA, STA)
            hot[partner, ROWS + r * PAIRS : ROWS + (r + 1) * PAIRS] = second[r * PAIRS : (r + 1) * PAIRS]
        return 0

    lax.fori_loop(0, STA, choose, 0)
    ramp = 8.0 / BINS

    for half in range(HALVES):
        for step in ORDER:
            bins_copy(half, step).wait()

        def pick(block, _):
            got = dot(hot[block], recv[half, block])
            u_buf[block] = got[0:ROWS]
            for r in range(ROUNDS):
                at = r * PAIRS
                v_buf[lax.rem(block + r, STA), at : at + PAIRS, :] = got[ROWS + at : ROWS + at + PAIRS]
            return 0

        lax.fori_loop(0, STA, pick, 0)
        start = s * WIDTH + half * HALF
        position = (lax.broadcasted_iota(jnp.int32, (1, HALF), 1) + start).astype(F32) + 0.5
        taper = jnp.minimum(1.0, jnp.minimum(position * ramp, (BINS - position) * ramp))

        def cross(n, _):
            block = lax.rem(s + 1 + n, STA)
            ur, ui = u_buf[block, :, 0:HALF], u_buf[block, :, HALF:]
            vr, vi = v_buf[block, :, 0:HALF], v_buf[block, :, HALF:]
            cr = ((ur * vr + ui * vi) * taper).astype(BF16)
            ci = ((ui * vr - ur * vi) * taper).astype(BF16)
            both = dot(jnp.concatenate([cr, ci], axis=1), forward_ref[half])
            y = both[:, 0 : 2 * RANK] + both[:, 2 * RANK :]
            if half > 0:
                y = y + y_sum[block]
            if half < HALVES - 1:
                y_sum[block] = y
                return 0
            rows = dot(spread_ref[...], y.astype(BF16)).astype(BF16)
            y_buf[pl.ds(block * DAY, DAY)] = rows.reshape(DAY, SLOT, 2 * RANK)

            def push(to, _):
                @pl.when(block * DAY + to != me)
                def _():
                    pltpu.make_async_remote_copy(
                        src_ref=y_buf.at[block * DAY + to], dst_ref=z_buf.at[me], send_sem=ssem, recv_sem=rsem,
                        device_id=(block, to), device_id_type=MESH,
                    ).start()
                return 0

            lax.fori_loop(0, DAY, push, 0)
            return 0

        lax.fori_loop(0, STA, cross, 0)

    z_buf[me] = y_buf[me]
    for t in range(TILES):
        table_copy(t).wait()
    rest = z_buf.at[pl.ds(0, DEVICES - 1)]
    pltpu.make_async_copy(rest, rest, ssem).wait()
    pltpu.make_async_copy(rest, rest, rsem).wait()

    sign = jnp.where(lax.broadcasted_iota(jnp.int32, (1, 2 * RANK), 1) < RANK, 1.0, -1.0)
    for block in range(STA):
        rows = z_buf[block * DAY : (block + 1) * DAY].reshape(DAY * SLOT, 2 * RANK)
        packed = lax.dot_general(spread_ref[...], rows, (((0,), (0,)), ((), ())), preferred_element_type=F32)
        at = block * 2 * RANK
        left[0:ROWS, at : at + 2 * RANK] = packed.astype(BF16)
        left[ROWS:, at : at + 2 * RANK] = (pltpu.roll(packed, RANK, 1) * sign).astype(BF16)
    group = 4 * MINE

    def tile(t, _):
        both = dot(left[...], table[t])
        re, im = both[0:ROWS], both[ROWS:]
        scale = jnp.minimum(lax.rsqrt(re * re + im * im), 4.0)
        for n, part in enumerate((re, re * scale, im * scale)):
            total = part[0:group]
            for g in range(1, ROWS // group):
                total = total + part[g * group : (g + 1) * group]
            sums[n] = total
        done = []
        for n in range(3):
            total = sums[n, 0:MINE, :]
            for g in range(1, 4):
                total = total + sums[n, g * MINE : (g + 1) * MINE, :]
            done.append(total * (1.0 / DAY))
        lags = pl.ds(pl.multiple_of(t * LAG_TILE, LAG_TILE), LAG_TILE)
        out_ref[:, lags] = done[0] * (done[1] * done[1] + done[2] * done[2])
        return 0

    lax.fori_loop(0, TILES, tile, 0)


def local(spectra, pair_stations):
    table, forward, spread = (jnp.asarray(a) for a in tables())
    vmem = pl.BlockSpec(memory_space=pltpu.VMEM)
    dma = pltpu.SemaphoreType.DMA
    return pl.pallas_call(
        correlate,
        name="correlate",
        out_shape=jax.ShapeDtypeStruct((MINE, LAGS), F32),
        in_specs=[vmem, vmem, vmem, vmem, pl.BlockSpec(memory_space=pl.ANY)],
        out_specs=vmem,
        scratch_shapes=[
            pltpu.VMEM((HALVES, STA, STATIONS, 2 * HALF), BF16),
            pltpu.VMEM((HALVES, STA, STATIONS, 2 * HALF), BF16),
            pltpu.VMEM((8, 256), jnp.int32),
            pltpu.VMEM((STA, 8, 256), jnp.int32),
            pltpu.VMEM((STA, 2 * ROWS, STATIONS), BF16),
            pltpu.VMEM((STA, ROWS, 2 * HALF), F32),
            pltpu.VMEM((STA, ROWS, 2 * HALF), F32),
            pltpu.VMEM((STA, ROWS, 2 * RANK), F32),
            pltpu.VMEM((DEVICES, SLOT, 2 * RANK), BF16),
            pltpu.VMEM((DEVICES, SLOT, 2 * RANK), BF16),
            pltpu.VMEM((2 * ROWS, STA * 2 * RANK), BF16),
            pltpu.VMEM((3, 4 * MINE, LAG_TILE), F32),
            pltpu.VMEM((TILES, STA * 2 * RANK, LAG_TILE), BF16),
            dma((HALVES, STA)),
            dma((HALVES, STA)),
            dma((STA,)),
            dma((STA,)),
            dma((TILES,)),
            dma,
            dma,
        ],
        compiler_params=pltpu.CompilerParams(collective_id=0, has_side_effects=True, vmem_limit_bytes=56 << 20),
    )(spectra.reshape(2, STATIONS, BINS), pair_stations.T, forward, spread, table)


def solution(mesh):
    placed = (P(None, "sta", "day", None), P("sta", None))
    return jax.shard_map(
        local, mesh=mesh, in_specs=placed, out_specs=P(("sta", "day"), None), check_vma=False
    )
```

time: 63.8 us -> 44.6 us (0.70)
  Pallas kernels: 63.6 us -> 42.8 us
  local copies, waits for them, and re-layouts: 0 us -> 1.67 us
    pallas_call x4 -> x1, Pallas kernels: 63.6 us -> 42.8 us  [local(): pl.pallas_call(correlate, name='correlate', out_shape=jax.ShapeDtypeStruc...]
    unnamed x0 -> x1, local copies, waits for them, and re-layouts: none -> 1.67 us
where the time goes in v2:
time: 44.6 us; the launch traced here: 44.5 us
  Pallas kernels  42.8 us (96%)
  local copies, waits for them, and re-layouts  1.67 us (4%)
    pallas_call x1, Pallas kernels, local(): pl.pallas_call(correlate, name='correlate', out_shape=jax.ShapeDtypeStruc...  42.8 us
    unnamed x1, local copies, waits for them, and re-layouts  1.67 us

profile of v2, /device:TPU:1, one launch (start us, length us, event | category | flops | bytes accessed | tf_op | source)
XLA Modules:
  0.0 44.5 jit_solution(8945832080867925469)
XLA Ops:
  0.0 42.8 %correlate.1 = f32[10,4096]{1,0:T(8,128)} custom-call(bf16[2,64,4096]{2,1,0:T(8,128)(2,1)} %bitcast.2, s32[2,160]{1,0:T(2,128)} %bitcast.3, bf16[2,512,256]{2,1,0:T(8,128)(2,1)} %constant.7.clone.forward_ref, bf16[256,160]{1,0:T(8,128)(2,1)} %constant.8.clone.spread_ref, bf16[8,1024,512]{2,1,0:T(8,128)(2,1)} %constant.6.clone.table_hbm), custom_call_target="tpu_custom_call" | custom-call | tf_op jit(solution)/shard_map/correlate/pallas_call | solution.py:246
  42.8 1.7 %copy.7 = f32[10,4096]{1,0:T(8,128)} copy(f32[10,4096]{1,0:T(8,128)} %correlate.1) | data formatting | bytes 327680

commit v3 on v2

v3 whole, which is shorter than its diff:
```python
import functools
import math

import numpy as np
import jax
import jax.numpy as jnp
import ml_dtypes
from jax import lax
from jax.experimental import pallas as pl
from jax.experimental.pallas import tpu as pltpu
from jax.sharding import PartitionSpec as P

BINS = 4096
LAGS = 4096
STA = 8
DAY = 16
STATIONS = 64
ROUNDS = 5
PAIRS = 32
ROWS = ROUNDS * PAIRS
MINE = ROWS // DAY
WIDTH = BINS // STA
RANK = 64
SLOT = 16
LAG_TILE = 512
TILES = LAGS // LAG_TILE
HALVES = 2
HALF = WIDTH // HALVES
DEVICES = STA * DAY
STEPS = range(1, STA)
FIRST_BIN = 36
PERIOD = 72000
MESH = pl.DeviceIdType.MESH
F32 = jnp.float32
BF16 = jnp.bfloat16


def prolate_basis(width, rank):
    t = np.arange(width, dtype=np.float64)
    half_band = LAGS / 2 / PERIOD
    diagonal = ((width - 1 - 2 * t) / 2) ** 2 * np.cos(2 * np.pi * half_band)
    off = t[1:] * (width - t[1:]) / 2
    matrix = np.diag(diagonal) + np.diag(off, 1) + np.diag(off, -1)
    _, vectors = np.linalg.eigh(matrix)
    vectors = vectors[:, ::-1][:, :rank]
    middle = width // 2
    signs = np.sign(vectors[middle])
    return vectors * signs[None]


@functools.lru_cache(maxsize=None)
def tables():
    basis = prolate_basis(WIDTH, RANK)
    lag = np.arange(LAGS, dtype=np.int64) - LAGS // 2
    rows = []
    for block in range(STA):
        bins = FIRST_BIN + block * WIDTH + np.arange(WIDTH, dtype=np.int64)
        turns = np.remainder(bins[:, None] * lag[None, :], PERIOD)
        angle = turns * (2.0 * np.pi / PERIOD)
        cosine, sine = np.cos(angle), np.sin(angle)
        rows.append(basis.T @ cosine)
        rows.append(-(basis.T @ sine))
    table = np.concatenate(rows, axis=0) / math.sqrt(BINS)
    table = table.reshape(STA * 2 * RANK, TILES, LAG_TILE).transpose(1, 0, 2)
    high = basis.astype(ml_dtypes.bfloat16).astype(np.float64)
    forward = np.zeros((HALVES, 2, HALF, 4, RANK))
    for half in range(HALVES):
        rows = slice(half * HALF, (half + 1) * HALF)
        for n, part in enumerate((high, basis - high)):
            forward[half, 0, :, 2 * n] = part[rows]
            forward[half, 1, :, 2 * n + 1] = part[rows]
    forward = forward.reshape(HALVES, 2 * HALF, 4 * RANK)
    spread = np.zeros((DAY * SLOT, ROWS))
    for row in range(ROWS):
        spread[row // MINE * SLOT + row % MINE, row] = 1.0
    as_bf16 = lambda a: np.ascontiguousarray(a).astype(ml_dtypes.bfloat16)
    return as_bf16(table), as_bf16(forward), as_bf16(spread), as_bf16(spread.T)


def dot(a, b):
    return jnp.dot(a, b, preferred_element_type=F32)


def correlate(x_hbm, idx_hbm, forward_hbm, spread_hbm, gather_hbm, table_hbm, out_ref,
              recv, pairs, hot, u_buf, v_buf, y_sum, y_buf, z_buf, left, sums, forward, spread, gather, table,
              wsem, wrsem, isem, irsem, osem, csem, tsem, ssem, rsem):
    s = lax.axis_index("sta")
    d = lax.axis_index("day")
    me = s * DAY + d

    barrier = pltpu.get_barrier_semaphore()
    for step in STEPS:
        pl.semaphore_signal(barrier, inc=1, device_id=(lax.rem(s + step, STA), d), device_id_type=MESH)
    for step in range(1, DAY):
        pl.semaphore_signal(barrier, inc=1, device_id=(s, lax.rem(d + step, DAY)), device_id_type=MESH)

    def bins_of(part, half):
        at = pl.multiple_of(part * WIDTH + half * HALF, HALF)
        return x_hbm.at[:, :, pl.ds(at, HALF)]

    def bins_copy(half, step):
        to = lax.rem(s + step, STA)
        return pltpu.make_async_remote_copy(
            src_ref=bins_of(to, half), dst_ref=recv.at[half, step],
            send_sem=wsem.at[half, step], recv_sem=wrsem.at[half, step],
            device_id=(to, d), device_id_type=MESH,
        )

    def pairs_copy(step):
        return pltpu.make_async_remote_copy(
            src_ref=idx_hbm, dst_ref=pairs.at[step], send_sem=isem.at[step], recv_sem=irsem.at[step],
            device_id=(lax.rem(s + step, STA), d), device_id_type=MESH,
        )

    own = [pltpu.make_async_copy(bins_of(s, half), recv.at[half, 0], osem.at[half]) for half in range(HALVES)]
    own.append(pltpu.make_async_copy(idx_hbm, pairs.at[0], osem.at[HALVES]))
    constants = [
        pltpu.make_async_copy(a, b, csem.at[n])
        for n, (a, b) in enumerate(((forward_hbm, forward), (spread_hbm, spread), (gather_hbm, gather)))
    ]
    tables_in = [pltpu.make_async_copy(table_hbm.at[t], table.at[t], tsem.at[t]) for t in range(TILES)]

    for copy in own:
        copy.start()
    pl.semaphore_wait(barrier, STA + DAY - 2)
    for step in STEPS:
        pairs_copy(step).start()
    for half in range(HALVES):
        for step in STEPS:
            bins_copy(half, step).start()
    for copy in constants + tables_in:
        copy.start()

    for step in STEPS:
        pairs_copy(step).wait()
    own[HALVES].wait()
    lanes = lax.broadcasted_iota(jnp.int32, (ROWS, STATIONS), 1)
    blank = jnp.zeros((8 - 2, ROWS), jnp.int32)
    for block in range(STA):
        rows = jnp.transpose(jnp.concatenate([pairs[block], blank], axis=0))
        hot[block, 0:ROWS] = jnp.where(rows[:, 0:1] == lanes, 1.0, 0.0).astype(BF16)
        second = jnp.where(rows[:, 1:2] == lanes, 1.0, 0.0).astype(BF16)
        for r in range(ROUNDS):
            at = r * PAIRS
            hot[(block + r) % STA, ROWS + at : ROWS + at + PAIRS] = second[at : at + PAIRS]
    for copy in constants:
        copy.wait()

    def pick(half, block):
        re = recv[half, block, 0].astype(F32)
        im = recv[half, block, 1].astype(F32)
        scale = jnp.minimum(lax.rsqrt(re * re + im * im), 4.0)
        for n, part in enumerate((re, im)):
            got = dot(hot[block], (part * scale).astype(BF16))
            u_buf[block, n] = got[0:ROWS]
            for r in range(ROUNDS):
                at = r * PAIRS
                v_buf[(block - r) % STA, n, at : at + PAIRS] = got[ROWS + at : ROWS + at + PAIRS]

    def cross(half, block, taper):
        ur, ui, vr, vi = u_buf[block, 0], u_buf[block, 1], v_buf[block, 0], v_buf[block, 1]
        cr = ((ur * vr + ui * vi) * taper).astype(BF16)
        ci = ((ui * vr - ur * vi) * taper).astype(BF16)
        both = dot(jnp.concatenate([cr, ci], axis=1), forward[half])
        y = both[:, 0 : 2 * RANK] + both[:, 2 * RANK :]
        if half > 0:
            y = y + y_sum[block]
        if half < HALVES - 1:
            y_sum[block] = y
        else:
            rows = dot(spread[...], y.astype(BF16)).astype(BF16)
            y_buf[block] = rows.reshape(DAY, SLOT, 2 * RANK)

    def push(block):
        other = lax.rem(s - block + STA, STA)
        for step in range(DAY):
            if block == 0 and step == 0:
                continue
            to = lax.rem(d + step, DAY)
            pltpu.make_async_remote_copy(
                src_ref=y_buf.at[block, to], dst_ref=z_buf.at[me], send_sem=ssem, recv_sem=rsem,
                device_id=(other, to), device_id_type=MESH,
            ).start()

    ramp = 8.0 / BINS
    for half in range(HALVES):
        for step in STEPS:
            bins_copy(half, step).wait()
        own[half].wait()
        for block in range(STA):
            pick(half, block)
        start = s * WIDTH + half * HALF
        position = (lax.broadcasted_iota(jnp.int32, (1, HALF), 1) + start).astype(F32) + 0.5
        taper = jnp.minimum(1.0, jnp.minimum(position * ramp, (BINS - position) * ramp))
        order = [n % STA for n in range(1, STA + 1)]
        for n, block in enumerate(order):
            cross(half, block, taper)
            if half == HALVES - 1 and n > 0:
                push(order[n - 1])
    push(order[-1])
    z_buf[me] = y_buf[0, d]

    for copy in tables_in:
        copy.wait()
    rest = z_buf.at[pl.ds(0, DEVICES - 1)]
    pltpu.make_async_copy(rest, rest, ssem).wait()
    pltpu.make_async_copy(rest, rest, rsem).wait()

    sign = jnp.where(lax.broadcasted_iota(jnp.int32, (1, 2 * RANK), 1) < RANK, 1.0, -1.0)
    for block in range(0, STA, 2):
        rows = [z_buf[n * DAY : (n + 1) * DAY].reshape(DAY * SLOT, 2 * RANK) for n in (block, block + 1)]
        packed = dot(gather[...], jnp.concatenate(rows, axis=1))
        for n in range(2):
            part = packed[:, n * 2 * RANK : (n + 1) * 2 * RANK]
            at = (block + n) * 2 * RANK
            left[0:ROWS, at : at + 2 * RANK] = part.astype(BF16)
            left[ROWS:, at : at + 2 * RANK] = (pltpu.roll(part, RANK, 1) * sign).astype(BF16)
    group = 4 * MINE

    for t in range(TILES):
        both = dot(left[...], table[t])
        re, im = both[0:ROWS], both[ROWS:]
        scale = jnp.minimum(lax.rsqrt(re * re + im * im), 4.0)
        done = []
        for n, part in enumerate((re, re * scale, im * scale)):
            total = part[0:group]
            for g in range(1, ROWS // group):
                total = total + part[g * group : (g + 1) * group]
            sums[t % 2, n] = total
            total = sums[t % 2, n, 0:MINE]
            for g in range(1, 4):
                total = total + sums[t % 2, n, g * MINE : (g + 1) * MINE]
            done.append(total * (1.0 / DAY))
        out_ref[:, t * LAG_TILE : (t + 1) * LAG_TILE] = done[0] * (done[1] * done[1] + done[2] * done[2])


def local(spectra, pair_stations):
    table, forward, spread, gather = (jnp.asarray(a) for a in tables())
    anywhere = pl.BlockSpec(memory_space=pl.ANY)
    dma = pltpu.SemaphoreType.DMA
    return pl.pallas_call(
        correlate,
        name="correlate",
        out_shape=jax.ShapeDtypeStruct((MINE, LAGS), F32),
        in_specs=[anywhere] * 6,
        out_specs=pl.BlockSpec(memory_space=pltpu.VMEM),
        scratch_shapes=[
            pltpu.VMEM((HALVES, STA, 2, STATIONS, HALF), BF16),
            pltpu.VMEM((STA, 2, ROWS), jnp.int32),
            pltpu.VMEM((STA, 2 * ROWS, STATIONS), BF16),
            pltpu.VMEM((STA, 2, ROWS, HALF), F32),
            pltpu.VMEM((STA, 2, ROWS, HALF), F32),
            pltpu.VMEM((STA, ROWS, 2 * RANK), F32),
            pltpu.VMEM((STA, DAY, SLOT, 2 * RANK), BF16),
            pltpu.VMEM((DEVICES, SLOT, 2 * RANK), BF16),
            pltpu.VMEM((2 * ROWS, STA * 2 * RANK), BF16),
            pltpu.VMEM((2, 3, 4 * MINE, LAG_TILE), F32),
            pltpu.VMEM((HALVES, 2 * HALF, 4 * RANK), BF16),
            pltpu.VMEM((DAY * SLOT, ROWS), BF16),
            pltpu.VMEM((ROWS, DAY * SLOT), BF16),
            pltpu.VMEM((TILES, STA * 2 * RANK, LAG_TILE), BF16),
            dma((HALVES, STA)),
            dma((HALVES, STA)),
            dma((STA,)),
            dma((STA,)),
            dma((HALVES + 1,)),
            dma((3,)),
            dma((TILES,)),
            dma,
            dma,
        ],
        compiler_params=pltpu.CompilerParams(collective_id=0, has_side_effects=True, vmem_limit_bytes=56 << 20),
    )(spectra.reshape(2, STATIONS, BINS), pair_stations.T, forward, spread, gather, table)


def solution(mesh):
    placed = (P(None, "sta", "day", None), P("sta", None))
    return jax.shard_map(
        local, mesh=mesh, in_specs=placed, out_specs=P(("sta", "day"), None), check_vma=False
    )
```

time: 44.6 us -> 41.6 us (0.933)
  Pallas kernels: 42.8 us -> 39.8 us
    pallas_call x1, Pallas kernels: 42.8 us -> 39.8 us  [local(): pl.pallas_call(correlate, name='correlate', out_shape=jax.ShapeDtypeStruc...]
where the time goes in v3:
time: 41.6 us; the launch traced here: 41.5 us
  Pallas kernels  39.8 us (96%)
  local copies, waits for them, and re-layouts  1.67 us (4%)
    pallas_call x1, Pallas kernels, local(): pl.pallas_call(correlate, name='correlate', out_shape=jax.ShapeDtypeStruc...  39.8 us
    unnamed x1, local copies, waits for them, and re-layouts  1.67 us

profile of v3, /device:TPU:1, one launch (start us, length us, event | category | flops | bytes accessed | tf_op | source)
XLA Modules:
  0.0 41.5 jit_solution(17990075955136097183)
XLA Ops:
  0.0 39.8 %correlate.1 = f32[10,4096]{1,0:T(8,128)} custom-call(bf16[2,64,4096]{2,1,0:T(8,128)(2,1)} %bitcast.2, s32[2,160]{1,0:T(2,128)} %bitcast.3, bf16[2,512,256]{2,1,0:T(8,128)(2,1)} %constant.9.clone.forward_hbm, bf16[256,160]{1,0:T(8,128)(2,1)} %constant.10.clone.spread_hbm, bf16[160,256]{1,0:T(8,128)(2,1)} %constant.11.clone.gather_hbm, ...), custom_call_target="tpu_custom_call" | custom-call | tf_op jit(solution)/shard_map/correlate/pallas_call | solution.py:241
  39.8 1.7 %copy.8 = f32[10,4096]{1,0:T(8,128)} copy(f32[10,4096]{1,0:T(8,128)} %correlate.1) | data formatting | bytes 327680

commit v4 on v3

--- a/solution.py
+++ b/solution.py
@@ -24,8 +24,9 @@
 SLOT = 16
 LAG_TILE = 512
 TILES = LAGS // LAG_TILE
-HALVES = 2
-HALF = WIDTH // HALVES
+CHUNKS = (384, 128)
+HALVES = len(CHUNKS)
+STARTS = tuple(sum(CHUNKS[:n]) for n in range(HALVES))
 DEVICES = STA * DAY
 STEPS = range(1, STA)
 FIRST_BIN = 36
@@ -63,13 +64,14 @@
     table = np.concatenate(rows, axis=0) / math.sqrt(BINS)
     table = table.reshape(STA * 2 * RANK, TILES, LAG_TILE).transpose(1, 0, 2)
     high = basis.astype(ml_dtypes.bfloat16).astype(np.float64)
-    forward = np.zeros((HALVES, 2, HALF, 4, RANK))
-    for half in range(HALVES):
-        rows = slice(half * HALF, (half + 1) * HALF)
+    forward = []
+    for start, width in zip(STARTS, CHUNKS):
+        piece = np.zeros((2, width, 4, RANK))
         for n, part in enumerate((high, basis - high)):
-            forward[half, 0, :, 2 * n] = part[rows]
-            forward[half, 1, :, 2 * n + 1] = part[rows]
-    forward = forward.reshape(HALVES, 2 * HALF, 4 * RANK)
+            piece[0, :, 2 * n] = part[start : start + width]
+            piece[1, :, 2 * n + 1] = part[start : start + width]
+        forward.append(piece.reshape(2 * width, 4 * RANK))
+    forward = np.concatenate(forward, axis=0)
     spread = np.zeros((DAY * SLOT, ROWS))
     for row in range(ROWS):
         spread[row // MINE * SLOT + row % MINE, row] = 1.0
@@ -95,13 +97,16 @@
         pl.semaphore_signal(barrier, inc=1, device_id=(s, lax.rem(d + step, DAY)), device_id_type=MESH)
 
     def bins_of(part, half):
-        at = pl.multiple_of(part * WIDTH + half * HALF, HALF)
-        return x_hbm.at[:, :, pl.ds(at, HALF)]
+        at = pl.multiple_of(part * WIDTH + STARTS[half], 128)
+        return x_hbm.at[:, :, pl.ds(at, CHUNKS[half])]
+
+    def landing(half, block):
+        return recv.at[block, :, :, STARTS[half] : STARTS[half] + CHUNKS[half]]
 
     def bins_copy(half, step):
         to = lax.rem(s + step, STA)
         return pltpu.make_async_remote_copy(
-            src_ref=bins_of(to, half), dst_ref=recv.at[half, step],
+            src_ref=bins_of(to, half), dst_ref=landing(half, step),
             send_sem=wsem.at[half, step], recv_sem=wrsem.at[half, step],
             device_id=(to, d), device_id_type=MESH,
         )
@@ -112,7 +117,7 @@
             device_id=(lax.rem(s + step, STA), d), device_id_type=MESH,
         )
 
-    own = [pltpu.make_async_copy(bins_of(s, half), recv.at[half, 0], osem.at[half]) for half in range(HALVES)]
+    own = [pltpu.make_async_copy(bins_of(s, half), landing(half, 0), osem.at[half]) for half in range(HALVES)]
     own.append(pltpu.make_async_copy(idx_hbm, pairs.at[0], osem.at[HALVES]))
     constants = [
         pltpu.make_async_copy(a, b, csem.at[n])
@@ -147,21 +152,21 @@
         copy.wait()
 
     def pick(half, block):
-        re = recv[half, block, 0].astype(F32)
-        im = recv[half, block, 1].astype(F32)
+        re = landing(half, block)[0].astype(F32)
+        im = landing(half, block)[1].astype(F32)
         scale = jnp.minimum(lax.rsqrt(re * re + im * im), 4.0)
         for n, part in enumerate((re, im)):
             got = dot(hot[block], (part * scale).astype(BF16))
-            u_buf[block, n] = got[0:ROWS]
+            u_buf[block, n, :, 0 : CHUNKS[half]] = got[0:ROWS]
             for r in range(ROUNDS):
                 at = r * PAIRS
-                v_buf[(block - r) % STA, n, at : at + PAIRS] = got[ROWS + at : ROWS + at + PAIRS]
+                v_buf[(block - r) % STA, n, at : at + PAIRS, 0 : CHUNKS[half]] = got[ROWS + at : ROWS + at + PAIRS]
 
     def cross(half, block, taper):
-        ur, ui, vr, vi = u_buf[block, 0], u_buf[block, 1], v_buf[block, 0], v_buf[block, 1]
+        ur, ui, vr, vi = (buf[block, n, :, 0 : CHUNKS[half]] for buf in (u_buf, v_buf) for n in range(2))
         cr = ((ur * vr + ui * vi) * taper).astype(BF16)
         ci = ((ui * vr - ur * vi) * taper).astype(BF16)
-        both = dot(jnp.concatenate([cr, ci], axis=1), forward[half])
+        both = dot(jnp.concatenate([cr, ci], axis=1), forward[2 * STARTS[half] : 2 * (STARTS[half] + CHUNKS[half])])
         y = both[:, 0 : 2 * RANK] + both[:, 2 * RANK :]
         if half > 0:
             y = y + y_sum[block]
@@ -173,14 +178,15 @@
 
     def push(block):
         other = lax.rem(s - block + STA, STA)
-        for step in range(DAY):
-            if block == 0 and step == 0:
-                continue
-            to = lax.rem(d + step, DAY)
-            pltpu.make_async_remote_copy(
+        for to in range(DAY):
+            copy = pltpu.make_async_remote_copy(
                 src_ref=y_buf.at[block, to], dst_ref=z_buf.at[me], send_sem=ssem, recv_sem=rsem,
                 device_id=(other, to), device_id_type=MESH,
-            ).start()
+            )
+            if block == 0:
+                pl.when(to != d)(copy.start)
+            else:
+                copy.start()
 
     ramp = 8.0 / BINS
     for half in range(HALVES):
@@ -189,15 +195,14 @@
         own[half].wait()
         for block in range(STA):
             pick(half, block)
-        start = s * WIDTH + half * HALF
-        position = (lax.broadcasted_iota(jnp.int32, (1, HALF), 1) + start).astype(F32) + 0.5
+        start = s * WIDTH + STARTS[half]
+        position = (lax.broadcasted_iota(jnp.int32, (1, CHUNKS[half]), 1) + start).astype(F32) + 0.5
         taper = jnp.minimum(1.0, jnp.minimum(position * ramp, (BINS - position) * ramp))
-        order = [n % STA for n in range(1, STA + 1)]
+        order = list(range(STA - 1, -1, -1))
         for n, block in enumerate(order):
             cross(half, block, taper)
-            if half == HALVES - 1 and n > 0:
-                push(order[n - 1])
-    push(order[-1])
+            if half == HALVES - 1:
+                push(block)
     z_buf[me] = y_buf[0, d]
 
     for copy in tables_in:
@@ -245,17 +250,17 @@
         in_specs=[anywhere] * 6,
         out_specs=pl.BlockSpec(memory_space=pltpu.VMEM),
         scratch_shapes=[
-            pltpu.VMEM((HALVES, STA, 2, STATIONS, HALF), BF16),
+            pltpu.VMEM((STA, 2, STATIONS, WIDTH), BF16),
             pltpu.VMEM((STA, 2, ROWS), jnp.int32),
             pltpu.VMEM((STA, 2 * ROWS, STATIONS), BF16),
-            pltpu.VMEM((STA, 2, ROWS, HALF), F32),
-            pltpu.VMEM((STA, 2, ROWS, HALF), F32),
+            pltpu.VMEM((STA, 2, ROWS, max(CHUNKS)), F32),
+            pltpu.VMEM((STA, 2, ROWS, max(CHUNKS)), F32),
             pltpu.VMEM((STA, ROWS, 2 * RANK), F32),
             pltpu.VMEM((STA, DAY, SLOT, 2 * RANK), BF16),
             pltpu.VMEM((DEVICES, SLOT, 2 * RANK), BF16),
             pltpu.VMEM((2 * ROWS, STA * 2 * RANK), BF16),
             pltpu.VMEM((2, 3, 4 * MINE, LAG_TILE), F32),
-            pltpu.VMEM((HALVES, 2 * HALF, 4 * RANK), BF16),
+            pltpu.VMEM((2 * WIDTH, 4 * RANK), BF16),
             pltpu.VMEM((DAY * SLOT, ROWS), BF16),
             pltpu.VMEM((ROWS, DAY * SLOT), BF16),
             pltpu.VMEM((TILES, STA * 2 * RANK, LAG_TILE), BF16),

time: 41.6 us -> 38.9 us (0.935)
  Pallas kernels: 39.8 us -> 37.1 us
    pallas_call x1, Pallas kernels: 39.8 us -> 37.1 us  [local(): pl.pallas_call(correlate, name='correlate', out_shape=jax.ShapeDtypeStruc...]
where the time goes in v4:
time: 38.9 us; the launch traced here: 38.8 us
  Pallas kernels  37.1 us (95%)
  local copies, waits for them, and re-layouts  1.67 us (4%)
    pallas_call x1, Pallas kernels, local(): pl.pallas_call(correlate, name='correlate', out_shape=jax.ShapeDtypeStruc...  37.1 us
    unnamed x1, local copies, waits for them, and re-layouts  1.67 us

profile of v4, /device:TPU:1, one launch (start us, length us, event | category | flops | bytes accessed | tf_op | source)
XLA Modules:
  0.0 38.8 jit_solution(6455572829889755860)
XLA Ops:
  0.0 37.1 %correlate.1 = f32[10,4096]{1,0:T(8,128)} custom-call(bf16[2,64,4096]{2,1,0:T(8,128)(2,1)} %bitcast.2, s32[2,160]{1,0:T(2,128)} %bitcast.3, bf16[1024,256]{1,0:T(8,128)(2,1)} %constant.9.clone.forward_hbm, bf16[256,160]{1,0:T(8,128)(2,1)} %constant.10.clone.spread_hbm, bf16[160,256]{1,0:T(8,128)(2,1)} %constant.11.clone.gather_hbm, ...), custom_call_target="tpu_custom_call" | custom-call | tf_op jit(solution)/shard_map/correlate/pallas_call | solution.py:246
  37.1 1.7 %copy.8 = f32[10,4096]{1,0:T(8,128)} copy(f32[10,4096]{1,0:T(8,128)} %correlate.1) | data formatting | bytes 327680

commit v5 on v4

--- a/solution.py
+++ b/solution.py
@@ -20,7 +20,11 @@
 ROWS = ROUNDS * PAIRS
 MINE = ROWS // DAY
 WIDTH = BINS // STA
-RANK = 64
+RANK = 48
+LANES = 64
+PIECE = LANES - RANK
+GROUP = 4
+DEPTH = 2 * (STA // GROUP) * (GROUP - 1) * LANES
 SLOT = 16
 LAG_TILE = 512
 TILES = LAGS // LAG_TILE
@@ -53,39 +57,44 @@
 def tables():
     basis = prolate_basis(WIDTH, RANK)
     lag = np.arange(LAGS, dtype=np.int64) - LAGS // 2
-    rows = []
+    blocks = []
     for block in range(STA):
         bins = FIRST_BIN + block * WIDTH + np.arange(WIDTH, dtype=np.int64)
         turns = np.remainder(bins[:, None] * lag[None, :], PERIOD)
         angle = turns * (2.0 * np.pi / PERIOD)
-        cosine, sine = np.cos(angle), np.sin(angle)
-        rows.append(basis.T @ cosine)
-        rows.append(-(basis.T @ sine))
+        blocks.append((basis.T @ np.cos(angle), -(basis.T @ np.sin(angle))))
+    rows = []
+    for group in range(0, STA, GROUP):
+        for n in range(GROUP - 1):
+            for part in range(2):
+                rows.append(blocks[group + n][part])
+                rows.append(blocks[group + GROUP - 1][part][n * PIECE : (n + 1) * PIECE])
     table = np.concatenate(rows, axis=0) / math.sqrt(BINS)
-    table = table.reshape(STA * 2 * RANK, TILES, LAG_TILE).transpose(1, 0, 2)
+    table = table.reshape(DEPTH, TILES, LAG_TILE).transpose(1, 0, 2).reshape(TILES * DEPTH, LAG_TILE)
     high = basis.astype(ml_dtypes.bfloat16).astype(np.float64)
     forward = []
     for start, width in zip(STARTS, CHUNKS):
-        piece = np.zeros((2, width, 4, RANK))
+        piece = np.zeros((2, width, 4, LANES))
         for n, part in enumerate((high, basis - high)):
-            piece[0, :, 2 * n] = part[start : start + width]
-            piece[1, :, 2 * n + 1] = part[start : start + width]
-        forward.append(piece.reshape(2 * width, 4 * RANK))
+            piece[0, :, 2 * n, 0:RANK] = part[start : start + width]
+            piece[1, :, 2 * n + 1, 0:RANK] = part[start : start + width]
+        forward.append(piece.reshape(2 * width, 4 * LANES))
     forward = np.concatenate(forward, axis=0)
     spread = np.zeros((DAY * SLOT, ROWS))
     for row in range(ROWS):
         spread[row // MINE * SLOT + row % MINE, row] = 1.0
-    as_bf16 = lambda a: np.ascontiguousarray(a).astype(ml_dtypes.bfloat16)
-    return as_bf16(table), as_bf16(forward), as_bf16(spread), as_bf16(spread.T)
+    spread = np.pad(spread, ((0, 0), (0, DAY * SLOT - ROWS)))
+    bank = [table, np.concatenate([forward[:WIDTH], forward[WIDTH:]], axis=1), np.concatenate([spread, spread.T], axis=1)]
+    return np.concatenate(bank, axis=0).astype(ml_dtypes.bfloat16)
 
 
 def dot(a, b):
     return jnp.dot(a, b, preferred_element_type=F32)
 
 
-def correlate(x_hbm, idx_hbm, forward_hbm, spread_hbm, gather_hbm, table_hbm, out_ref,
+def correlate(x_hbm, idx_hbm, bank_hbm, out_ref,
               recv, pairs, hot, u_buf, v_buf, y_sum, y_buf, z_buf, left, sums, forward, spread, gather, table,
-              wsem, wrsem, isem, irsem, osem, csem, tsem, ssem, rsem):
+              wsem, wrsem, isem, irsem, osem, csem, ssem, rsem):
     s = lax.axis_index("sta")
     d = lax.axis_index("day")
     me = s * DAY + d
@@ -119,11 +128,19 @@
 
     own = [pltpu.make_async_copy(bins_of(s, half), landing(half, 0), osem.at[half]) for half in range(HALVES)]
     own.append(pltpu.make_async_copy(idx_hbm, pairs.at[0], osem.at[HALVES]))
+    def bank_copy(row, column, target, n):
+        source = bank_hbm.at[row : row + target.shape[0], column : column + target.shape[1]]
+        return pltpu.make_async_copy(source, target, csem.at[n])
+
+    side = LAG_TILE // 2
+    base = TILES * DEPTH
+    tables_in = [bank_copy(t * DEPTH, 0, table.at[t], t) for t in range(TILES)]
     constants = [
-        pltpu.make_async_copy(a, b, csem.at[n])
-        for n, (a, b) in enumerate(((forward_hbm, forward), (spread_hbm, spread), (gather_hbm, gather)))
+        bank_copy(base, 0, forward.at[0:WIDTH], TILES),
+        bank_copy(base, side, forward.at[WIDTH : 2 * WIDTH], TILES + 1),
+        bank_copy(base + WIDTH, 0, spread, TILES + 2),
+        bank_copy(base + WIDTH, side, gather, TILES + 3),
     ]
-    tables_in = [pltpu.make_async_copy(table_hbm.at[t], table.at[t], tsem.at[t]) for t in range(TILES)]
 
     for copy in own:
         copy.start()
@@ -155,8 +172,9 @@
         re = landing(half, block)[0].astype(F32)
         im = landing(half, block)[1].astype(F32)
         scale = jnp.minimum(lax.rsqrt(re * re + im * im), 4.0)
-        for n, part in enumerate((re, im)):
-            got = dot(hot[block], (part * scale).astype(BF16))
+        both = dot(hot[block], jnp.concatenate([re * scale, im * scale], axis=1).astype(BF16))
+        for n in range(2):
+            got = both[:, n * CHUNKS[half] : (n + 1) * CHUNKS[half]]
             u_buf[block, n, :, 0 : CHUNKS[half]] = got[0:ROWS]
             for r in range(ROUNDS):
                 at = r * PAIRS
@@ -167,14 +185,14 @@
         cr = ((ur * vr + ui * vi) * taper).astype(BF16)
         ci = ((ui * vr - ur * vi) * taper).astype(BF16)
         both = dot(jnp.concatenate([cr, ci], axis=1), forward[2 * STARTS[half] : 2 * (STARTS[half] + CHUNKS[half])])
-        y = both[:, 0 : 2 * RANK] + both[:, 2 * RANK :]
+        y = both[:, 0 : 2 * LANES] + both[:, 2 * LANES :]
         if half > 0:
             y = y + y_sum[block]
         if half < HALVES - 1:
             y_sum[block] = y
         else:
-            rows = dot(spread[...], y.astype(BF16)).astype(BF16)
-            y_buf[block] = rows.reshape(DAY, SLOT, 2 * RANK)
+            rows = dot(spread[:, 0:ROWS], y.astype(BF16)).astype(BF16)
+            y_buf[block] = rows.reshape(DAY, SLOT, 2 * LANES)
 
     def push(block):
         other = lax.rem(s - block + STA, STA)
@@ -211,15 +229,20 @@
     pltpu.make_async_copy(rest, rest, ssem).wait()
     pltpu.make_async_copy(rest, rest, rsem).wait()
 
-    sign = jnp.where(lax.broadcasted_iota(jnp.int32, (1, 2 * RANK), 1) < RANK, 1.0, -1.0)
+    lane = lax.broadcasted_iota(jnp.int32, (1, 2 * LANES), 1)
+    sign = jnp.where(lane < LANES, 1.0, -1.0)
+    free = lax.rem(lane, LANES) >= RANK
+    parts = []
     for block in range(0, STA, 2):
-        rows = [z_buf[n * DAY : (n + 1) * DAY].reshape(DAY * SLOT, 2 * RANK) for n in (block, block + 1)]
-        packed = dot(gather[...], jnp.concatenate(rows, axis=1))
-        for n in range(2):
-            part = packed[:, n * 2 * RANK : (n + 1) * 2 * RANK]
-            at = (block + n) * 2 * RANK
-            left[0:ROWS, at : at + 2 * RANK] = part.astype(BF16)
-            left[ROWS:, at : at + 2 * RANK] = (pltpu.roll(part, RANK, 1) * sign).astype(BF16)
+        rows = [z_buf[n * DAY : (n + 1) * DAY].reshape(DAY * SLOT, 2 * LANES) for n in (block, block + 1)]
+        packed = dot(gather[0:ROWS], jnp.concatenate(rows, axis=1))
+        parts += [packed[:, 0 : 2 * LANES], packed[:, 2 * LANES :]]
+    for g in range(0, STA, GROUP):
+        for n in range(GROUP - 1):
+            part = jnp.where(free, pltpu.roll(parts[g + GROUP - 1], RANK - n * PIECE, 1), parts[g + n])
+            at = (g // GROUP * (GROUP - 1) + n) * 2 * LANES
+            left[0:ROWS, at : at + 2 * LANES] = part.astype(BF16)
+            left[ROWS:, at : at + 2 * LANES] = (pltpu.roll(part, LANES, 1) * sign).astype(BF16)
     group = 4 * MINE
 
     for t in range(TILES):
@@ -240,14 +263,14 @@
 
 
 def local(spectra, pair_stations):
-    table, forward, spread, gather = (jnp.asarray(a) for a in tables())
+    bank = jnp.asarray(tables())
     anywhere = pl.BlockSpec(memory_space=pl.ANY)
     dma = pltpu.SemaphoreType.DMA
     return pl.pallas_call(
         correlate,
         name="correlate",
         out_shape=jax.ShapeDtypeStruct((MINE, LAGS), F32),
-        in_specs=[anywhere] * 6,
+        in_specs=[anywhere] * 3,
         out_specs=pl.BlockSpec(memory_space=pltpu.VMEM),
         scratch_shapes=[
             pltpu.VMEM((STA, 2, STATIONS, WIDTH), BF16),
@@ -255,27 +278,26 @@
             pltpu.VMEM((STA, 2 * ROWS, STATIONS), BF16),
             pltpu.VMEM((STA, 2, ROWS, max(CHUNKS)), F32),
             pltpu.VMEM((STA, 2, ROWS, max(CHUNKS)), F32),
-            pltpu.VMEM((STA, ROWS, 2 * RANK), F32),
-            pltpu.VMEM((STA, DAY, SLOT, 2 * RANK), BF16),
-            pltpu.VMEM((DEVICES, SLOT, 2 * RANK), BF16),
-            pltpu.VMEM((2 * ROWS, STA * 2 * RANK), BF16),
+            pltpu.VMEM((STA, ROWS, 2 * LANES), F32),
+            pltpu.VMEM((STA, DAY, SLOT, 2 * LANES), BF16),
+            pltpu.VMEM((DEVICES, SLOT, 2 * LANES), BF16),
+            pltpu.VMEM((2 * ROWS, DEPTH), BF16),
             pltpu.VMEM((2, 3, 4 * MINE, LAG_TILE), F32),
-            pltpu.VMEM((2 * WIDTH, 4 * RANK), BF16),
-            pltpu.VMEM((DAY * SLOT, ROWS), BF16),
-            pltpu.VMEM((ROWS, DAY * SLOT), BF16),
-            pltpu.VMEM((TILES, STA * 2 * RANK, LAG_TILE), BF16),
+            pltpu.VMEM((2 * WIDTH, 4 * LANES), BF16),
+            pltpu.VMEM((DAY * SLOT, DAY * SLOT), BF16),
+            pltpu.VMEM((DAY * SLOT, DAY * SLOT), BF16),
+            pltpu.VMEM((TILES, DEPTH, LAG_TILE), BF16),
             dma((HALVES, STA)),
             dma((HALVES, STA)),
             dma((STA,)),
             dma((STA,)),
             dma((HALVES + 1,)),
-            dma((3,)),
-            dma((TILES,)),
+            dma((TILES + 4,)),
             dma,
             dma,
         ],
-        compiler_params=pltpu.CompilerParams(collective_id=0, has_side_effects=True, vmem_limit_bytes=56 << 20),
-    )(spectra.reshape(2, STATIONS, BINS), pair_stations.T, forward, spread, gather, table)
+        compiler_params=pltpu.CompilerParams(collective_id=0, has_side_effects=True, vmem_limit_bytes=107 << 19),
+    )(spectra.reshape(2, STATIONS, BINS), pair_stations.T, bank)
 
 
 def solution(mesh):

time: 38.9 us -> 37.1 us (0.954)
  Pallas kernels: 37.1 us -> 35.6 us
    pallas_call x1, Pallas kernels: 37.1 us -> 35.6 us  [local(): pl.pallas_call(correlate, name='correlate', out_shape=jax.ShapeDtypeStruc...]
    unnamed x1 -> x3, local copies, waits for them, and re-layouts: 1.67 us -> 1.39 us
where the time goes in v5:
time: 37.1 us; the launch traced here: 37 us
  Pallas kernels  35.6 us (96%)
  local copies, waits for them, and re-layouts  1.39 us (4%)
    pallas_call x1, Pallas kernels, local(): pl.pallas_call(correlate, name='correlate', out_shape=jax.ShapeDtypeStruc...  35.6 us
    unnamed x3, local copies, waits for them, and re-layouts  1.39 us

profile of v5, /device:TPU:1, one launch (start us, length us, event | category | flops | bytes accessed | tf_op | source)
XLA Modules:
  0.0 37.0 jit_solution(17728017723228596936)
XLA Ops:
  0.0 0.0 copy-start
  0.0 0.7 %copy-done = s32[160,2]{0,1:T(2,128)S(1)} copy-done((s32[160,2]{0,1:T(2,128)S(1)}, s32[160,2]{0,1:T(2,128)}, u32[]{:S(2)}) %copy-start) | copy-done | bytes 1304
  0.7 35.6 %correlate.1 = f32[10,4096]{1,0:T(8,128)S(1)} custom-call(bf16[2,64,4096]{2,1,0:T(8,128)(2,1)} %bitcast.3, s32[2,160]{1,0:T(2,128)S(1)} %bitcast.2, bf16[6912,512]{1,0:T(8,128)(2,1)} %constant.2.clone.bank_hbm), custom_call_target="tpu_custom_call" | custom-call | tf_op jit(solution)/shard_map/correlate/pallas_call | solution.py:269
  36.3 0.7 %copy.5 = f32[10,4096]{1,0:T(8,128)} copy(f32[10,4096]{1,0:T(8,128)S(1)} %correlate.1) | data formatting | bytes 327680
Async XLA Ops:
  0.0 0.7 %copy-start = (s32[160,2]{0,1:T(2,128)S(1)}, s32[160,2]{0,1:T(2,128)}, u32[]{:S(2)}) copy-start(s32[160,2]{0,1:T(2,128)} %param.4) | copy-start | bytes 3844

commit v6 on v5

--- a/solution.py
+++ b/solution.py
@@ -80,11 +80,10 @@
             piece[1, :, 2 * n + 1, 0:RANK] = part[start : start + width]
         forward.append(piece.reshape(2 * width, 4 * LANES))
     forward = np.concatenate(forward, axis=0)
-    spread = np.zeros((DAY * SLOT, ROWS))
+    gather = np.zeros((DAY * SLOT, LAG_TILE))
     for row in range(ROWS):
-        spread[row // MINE * SLOT + row % MINE, row] = 1.0
-    spread = np.pad(spread, ((0, 0), (0, DAY * SLOT - ROWS)))
-    bank = [table, np.concatenate([forward[:WIDTH], forward[WIDTH:]], axis=1), np.concatenate([spread, spread.T], axis=1)]
+        gather[row, row // MINE * SLOT + row % MINE] = 1.0
+    bank = [table, np.concatenate([forward[:WIDTH], forward[WIDTH:]], axis=1), gather]
     return np.concatenate(bank, axis=0).astype(ml_dtypes.bfloat16)
 
 
@@ -93,7 +92,7 @@
 
 
 def correlate(x_hbm, idx_hbm, bank_hbm, out_ref,
-              recv, pairs, hot, u_buf, v_buf, y_sum, y_buf, z_buf, left, sums, forward, spread, gather, table,
+              recv, pairs, hot, u_buf, v_buf, y_sum, y_buf, z_buf, left, sums, forward, gather, table,
               wsem, wrsem, isem, irsem, osem, csem, ssem, rsem):
     s = lax.axis_index("sta")
     d = lax.axis_index("day")
@@ -138,8 +137,7 @@
     constants = [
         bank_copy(base, 0, forward.at[0:WIDTH], TILES),
         bank_copy(base, side, forward.at[WIDTH : 2 * WIDTH], TILES + 1),
-        bank_copy(base + WIDTH, 0, spread, TILES + 2),
-        bank_copy(base + WIDTH, side, gather, TILES + 3),
+        bank_copy(base + WIDTH, 0, gather, TILES + 2),
     ]
 
     for copy in own:
@@ -156,6 +154,7 @@
     for step in STEPS:
         pairs_copy(step).wait()
     own[HALVES].wait()
+    y_sum[:, ROWS:, :] = jnp.zeros((STA, SLOT, 2 * LANES), F32)
     lanes = lax.broadcasted_iota(jnp.int32, (ROWS, STATIONS), 1)
     blank = jnp.zeros((8 - 2, ROWS), jnp.int32)
     for block in range(STA):
@@ -187,12 +186,13 @@
         both = dot(jnp.concatenate([cr, ci], axis=1), forward[2 * STARTS[half] : 2 * (STARTS[half] + CHUNKS[half])])
         y = both[:, 0 : 2 * LANES] + both[:, 2 * LANES :]
         if half > 0:
-            y = y + y_sum[block]
+            y = y + y_sum[block, 0:ROWS]
         if half < HALVES - 1:
-            y_sum[block] = y
+            y_sum[block, 0:ROWS] = y
         else:
-            rows = dot(spread[:, 0:ROWS], y.astype(BF16)).astype(BF16)
-            y_buf[block] = rows.reshape(DAY, SLOT, 2 * LANES)
+            y_sum[block, 0:ROWS] = y
+            for to in range(DAY):
+                y_buf[block, to] = y_sum[block, to * MINE : to * MINE + SLOT].astype(BF16)
 
     def push(block):
         other = lax.rem(s - block + STA, STA)
@@ -219,14 +219,14 @@
         order = list(range(STA - 1, -1, -1))
         for n, block in enumerate(order):
             cross(half, block, taper)
-            if half == HALVES - 1:
-                push(block)
+            if half == HALVES - 1 and n > 0:
+                push(order[n - 1])
+    push(order[-1])
     z_buf[me] = y_buf[0, d]
 
     for copy in tables_in:
         copy.wait()
     rest = z_buf.at[pl.ds(0, DEVICES - 1)]
-    pltpu.make_async_copy(rest, rest, ssem).wait()
     pltpu.make_async_copy(rest, rest, rsem).wait()
 
     lane = lax.broadcasted_iota(jnp.int32, (1, 2 * LANES), 1)
@@ -260,6 +260,7 @@
                 total = total + sums[t % 2, n, g * MINE : (g + 1) * MINE]
             done.append(total * (1.0 / DAY))
         out_ref[:, t * LAG_TILE : (t + 1) * LAG_TILE] = done[0] * (done[1] * done[1] + done[2] * done[2])
+    pltpu.make_async_copy(rest, rest, ssem).wait()
 
 
 def local(spectra, pair_stations):
@@ -278,13 +279,12 @@
             pltpu.VMEM((STA, 2 * ROWS, STATIONS), BF16),
             pltpu.VMEM((STA, 2, ROWS, max(CHUNKS)), F32),
             pltpu.VMEM((STA, 2, ROWS, max(CHUNKS)), F32),
-            pltpu.VMEM((STA, ROWS, 2 * LANES), F32),
+            pltpu.VMEM((STA, ROWS + SLOT, 2 * LANES), F32),
             pltpu.VMEM((STA, DAY, SLOT, 2 * LANES), BF16),
             pltpu.VMEM((DEVICES, SLOT, 2 * LANES), BF16),
             pltpu.VMEM((2 * ROWS, DEPTH), BF16),
             pltpu.VMEM((2, 3, 4 * MINE, LAG_TILE), F32),
             pltpu.VMEM((2 * WIDTH, 4 * LANES), BF16),
-            pltpu.VMEM((DAY * SLOT, DAY * SLOT), BF16),
             pltpu.VMEM((DAY * SLOT, DAY * SLOT), BF16),
             pltpu.VMEM((TILES, DEPTH, LAG_TILE), BF16),
             dma((HALVES, STA)),
@@ -292,7 +292,7 @@
             dma((STA,)),
             dma((STA,)),
             dma((HALVES + 1,)),
-            dma((TILES + 4,)),
+            dma((TILES + 3,)),
             dma,
             dma,
         ],

time: 37.1 us -> 36.7 us (0.989)
  Pallas kernels: 35.6 us -> 35.2 us
    pallas_call x1, Pallas kernels: 35.6 us -> 35.2 us  [local(): pl.pallas_call(correlate, name='correlate', out_shape=jax.ShapeDtypeStruc...]
where the time goes in v6:
time: 36.7 us; the launch traced here: 36.6 us
  Pallas kernels  35.2 us (96%)
  local copies, waits for them, and re-layouts  1.39 us (4%)
    pallas_call x1, Pallas kernels, local(): pl.pallas_call(correlate, name='correlate', out_shape=jax.ShapeDtypeStruc...  35.2 us
    unnamed x3, local copies, waits for them, and re-layouts  1.39 us

profile of v6, /device:TPU:1, one launch (start us, length us, event | category | flops | bytes accessed | tf_op | source)
XLA Modules:
  0.0 36.6 jit_solution(3831480725303751617)
XLA Ops:
  0.0 0.0 copy-start
  0.0 0.7 %copy-done = s32[160,2]{0,1:T(2,128)S(1)} copy-done((s32[160,2]{0,1:T(2,128)S(1)}, s32[160,2]{0,1:T(2,128)}, u32[]{:S(2)}) %copy-start) | copy-done | bytes 1304
  0.7 35.2 %correlate.1 = f32[10,4096]{1,0:T(8,128)S(1)} custom-call(bf16[2,64,4096]{2,1,0:T(8,128)(2,1)} %bitcast.3, s32[2,160]{1,0:T(2,128)S(1)} %bitcast.2, bf16[6912,512]{1,0:T(8,128)(2,1)} %constant.2.clone.bank_hbm), custom_call_target="tpu_custom_call" | custom-call | tf_op jit(solution)/shard_map/correlate/pallas_call | solution.py:270
  35.9 0.7 %copy.5 = f32[10,4096]{1,0:T(8,128)} copy(f32[10,4096]{1,0:T(8,128)S(1)} %correlate.1) | data formatting | bytes 327680
Async XLA Ops:
  0.0 0.7 %copy-start = (s32[160,2]{0,1:T(2,128)S(1)}, s32[160,2]{0,1:T(2,128)}, u32[]{:S(2)}) copy-start(s32[160,2]{0,1:T(2,128)} %param.4) | copy-start | bytes 3844

commit v7 on v6

--- a/solution.py
+++ b/solution.py
@@ -80,10 +80,7 @@
             piece[1, :, 2 * n + 1, 0:RANK] = part[start : start + width]
         forward.append(piece.reshape(2 * width, 4 * LANES))
     forward = np.concatenate(forward, axis=0)
-    gather = np.zeros((DAY * SLOT, LAG_TILE))
-    for row in range(ROWS):
-        gather[row, row // MINE * SLOT + row % MINE] = 1.0
-    bank = [table, np.concatenate([forward[:WIDTH], forward[WIDTH:]], axis=1), gather]
+    bank = [table, np.concatenate([forward[:WIDTH], forward[WIDTH:]], axis=1)]
     return np.concatenate(bank, axis=0).astype(ml_dtypes.bfloat16)
 
 
@@ -92,7 +89,7 @@
 
 
 def correlate(x_hbm, idx_hbm, bank_hbm, out_ref,
-              recv, pairs, hot, u_buf, v_buf, y_sum, y_buf, z_buf, left, sums, forward, gather, table,
+              recv, pairs, hot, u_buf, v_buf, y_sum, y_buf, z_buf, left, sums, forward, table,
               wsem, wrsem, isem, irsem, osem, csem, ssem, rsem):
     s = lax.axis_index("sta")
     d = lax.axis_index("day")
@@ -137,7 +134,6 @@
     constants = [
         bank_copy(base, 0, forward.at[0:WIDTH], TILES),
         bank_copy(base, side, forward.at[WIDTH : 2 * WIDTH], TILES + 1),
-        bank_copy(base + WIDTH, 0, gather, TILES + 2),
     ]
 
     for copy in own:
@@ -233,10 +229,10 @@
     sign = jnp.where(lane < LANES, 1.0, -1.0)
     free = lax.rem(lane, LANES) >= RANK
     parts = []
-    for block in range(0, STA, 2):
-        rows = [z_buf[n * DAY : (n + 1) * DAY].reshape(DAY * SLOT, 2 * LANES) for n in (block, block + 1)]
-        packed = dot(gather[0:ROWS], jnp.concatenate(rows, axis=1))
-        parts += [packed[:, 0 : 2 * LANES], packed[:, 2 * LANES :]]
+    for block in range(STA):
+        for day in range(DAY):
+            y_sum[block, day * MINE : day * MINE + SLOT] = z_buf[block * DAY + day].astype(F32)
+        parts.append(y_sum[block, 0:ROWS])
     for g in range(0, STA, GROUP):
         for n in range(GROUP - 1):
             part = jnp.where(free, pltpu.roll(parts[g + GROUP - 1], RANK - n * PIECE, 1), parts[g + n])
@@ -285,14 +281,13 @@
             pltpu.VMEM((2 * ROWS, DEPTH), BF16),
             pltpu.VMEM((2, 3, 4 * MINE, LAG_TILE), F32),
             pltpu.VMEM((2 * WIDTH, 4 * LANES), BF16),
-            pltpu.VMEM((DAY * SLOT, DAY * SLOT), BF16),
             pltpu.VMEM((TILES, DEPTH, LAG_TILE), BF16),
             dma((HALVES, STA)),
             dma((HALVES, STA)),
             dma((STA,)),
             dma((STA,)),
             dma((HALVES + 1,)),
-            dma((TILES + 3,)),
+            dma((TILES + 2,)),
             dma,
             dma,
         ],

time: 36.7 us -> 36.6 us (level)
  no operation moved by 1% of the time
where the time goes in v7:
time: 36.6 us; the launch traced here: 36.5 us
  Pallas kernels  35.1 us (96%)
  local copies, waits for them, and re-layouts  1.39 us (4%)
    pallas_call x1, Pallas kernels, local(): pl.pallas_call(correlate, name='correlate', out_shape=jax.ShapeDtypeStruc...  35.1 us
    unnamed x3, local copies, waits for them, and re-layouts  1.39 us

profile of v7, /device:TPU:1, one launch (start us, length us, event | category | flops | bytes accessed | tf_op | source)
XLA Modules:
  0.0 36.5 jit_solution(3740666700791224738)
XLA Ops:
  0.0 0.0 copy-start
  0.0 0.7 %copy-done = s32[160,2]{0,1:T(2,128)S(1)} copy-done((s32[160,2]{0,1:T(2,128)S(1)}, s32[160,2]{0,1:T(2,128)}, u32[]{:S(2)}) %copy-start) | copy-done | bytes 1304
  0.7 35.1 %correlate.1 = f32[10,4096]{1,0:T(8,128)S(1)} custom-call(bf16[2,64,4096]{2,1,0:T(8,128)(2,1)} %bitcast.3, s32[2,160]{1,0:T(2,128)S(1)} %bitcast.2, bf16[6656,512]{1,0:T(8,128)(2,1)} %constant.2.clone.bank_hbm), custom_call_target="tpu_custom_call" | custom-call | tf_op jit(solution)/shard_map/correlate/pallas_call | solution.py:266
  35.8 0.7 %copy.5 = f32[10,4096]{1,0:T(8,128)} copy(f32[10,4096]{1,0:T(8,128)S(1)} %correlate.1) | data formatting | bytes 327680
Async XLA Ops:
  0.0 0.7 %copy-start = (s32[160,2]{0,1:T(2,128)S(1)}, s32[160,2]{0,1:T(2,128)}, u32[]{:S(2)}) copy-start(s32[160,2]{0,1:T(2,128)} %param.4) | copy-start | bytes 3844

commit v8 on v6

--- a/solution.py
+++ b/solution.py
@@ -28,7 +28,7 @@
 SLOT = 16
 LAG_TILE = 512
 TILES = LAGS // LAG_TILE
-CHUNKS = (384, 128)
+CHUNKS = (256, 128, 128)
 HALVES = len(CHUNKS)
 STARTS = tuple(sum(CHUNKS[:n]) for n in range(HALVES))
 DEVICES = STA * DAY

time: 36.7 us -> 36.7 us (level)
  no operation moved by 1% of the time
where the time goes in v8:
time: 36.7 us; the launch traced here: 36.6 us
  Pallas kernels  35.2 us (96%)
  local copies, waits for them, and re-layouts  1.39 us (4%)
    pallas_call x1, Pallas kernels, local(): pl.pallas_call(correlate, name='correlate', out_shape=jax.ShapeDtypeStruc...  35.2 us
    unnamed x3, local copies, waits for them, and re-layouts  1.39 us

profile of v8, /device:TPU:1, one launch (start us, length us, event | category | flops | bytes accessed | tf_op | source)
XLA Modules:
  0.0 36.6 jit_solution(4444528816295067042)
XLA Ops:
  0.0 0.0 copy-start
  0.0 0.7 %copy-done = s32[160,2]{0,1:T(2,128)S(1)} copy-done((s32[160,2]{0,1:T(2,128)S(1)}, s32[160,2]{0,1:T(2,128)}, u32[]{:S(2)}) %copy-start) | copy-done | bytes 1304
  0.7 35.2 %correlate.1 = f32[10,4096]{1,0:T(8,128)S(1)} custom-call(bf16[2,64,4096]{2,1,0:T(8,128)(2,1)} %bitcast.3, s32[2,160]{1,0:T(2,128)S(1)} %bitcast.2, bf16[6912,512]{1,0:T(8,128)(2,1)} %constant.2.clone.bank_hbm), custom_call_target="tpu_custom_call" | custom-call | tf_op jit(solution)/shard_map/correlate/pallas_call | solution.py:270
  35.9 0.7 %copy.5 = f32[10,4096]{1,0:T(8,128)} copy(f32[10,4096]{1,0:T(8,128)S(1)} %correlate.1) | data formatting | bytes 327680
Async XLA Ops:
  0.0 0.7 %copy-start = (s32[160,2]{0,1:T(2,128)S(1)}, s32[160,2]{0,1:T(2,128)}, u32[]{:S(2)}) copy-start(s32[160,2]{0,1:T(2,128)} %param.4) | copy-start | bytes 3844
